TPU v7x, 32 devices: a whole 2x2x4 slice. The times are simulated.
32 devices in a mesh: fsdp: 4 (over z), ctx: 2 (over x), tp: 4 (over y, core).
Axes of the slice: x: 2, y: 2, z: 4, core: 2. Of those that a mesh axis runs over, the one named last changes fastest.
Arguments:
- tokens: bfloat16 [4, 1024, 1024], P('fsdp', 'ctx'), may hold values from -6 to 6
- lengths: int32 [4], P('fsdp'), may hold values from 512 to 1024, as said below
- cotangent: bfloat16 [4, 1024, 1024], P('fsdp', 'ctx'), may hold values from -6 to 6
- in_norm_gain: bfloat16 [1024], P(('fsdp', 'ctx')), may hold values from 0.5 to 1.5
- ffn_norm_gain: bfloat16 [1024], P(('fsdp', 'ctx')), may hold values from 0.099609375 to 1.8984375
- mixer_in: bfloat16 [1024, 2, 1536], P(('fsdp', 'ctx'), None, 'tp'), may hold values from -0.1875 to 0.1875
- step_weight: bfloat16 [1024, 24], P(('fsdp', 'ctx'), 'tp'), may hold values from -0.1875 to 0.1875
- state_proj: bfloat16 [1024, 256], P(('fsdp', 'ctx')), may hold values from -0.0078125 to 0.0078125
- keyval_weight: bfloat16 [1024, 256], P(('fsdp', 'ctx')), may hold values from -0.1875 to 0.1875
- query_weight: bfloat16 [1024, 512], P(('fsdp', 'ctx'), 'tp'), may hold values from -0.1875 to 0.1875
- step_bias: float32 [24], P('tp'), may hold values from -2 to 1
- decay_log: float32 [24], P('tp'), may hold values from -12 to -2.5
- skip_gain: float32 [24], P('tp'), may hold values from 0.5 to 1.5
- mixer_out: bfloat16 [1536, 1024], P('tp', ('fsdp', 'ctx')), may hold values from -0.15625 to 0.15625
- attn_out: bfloat16 [512, 1024], P('tp', ('fsdp', 'ctx')), may hold values from -0.75 to 0.75
- ffn_gate: bfloat16 [1024, 2048], P(('fsdp', 'ctx'), 'tp'), may hold values from -0.1875 to 0.1875
- ffn_up: bfloat16 [1024, 2048], P(('fsdp', 'ctx'), 'tp'), may hold values from -0.1875 to 0.1875
- ffn_down: bfloat16 [2048, 1024], P('tp', ('fsdp', 'ctx')), may hold values from -0.25 to 0.25
Outputs:
- block_out: bfloat16 [4, 1024, 1024], P('fsdp', 'ctx')
- input_grad: float32 [4, 1024, 1024], P('fsdp', 'ctx')
- in_norm_grad: float32 [1024], P(('fsdp', 'ctx'))
- ffn_norm_grad: float32 [1024], P(('fsdp', 'ctx'))
- mixer_in_grad: float32 [1024, 2, 1536], P(('fsdp', 'ctx'), None, 'tp')
- step_weight_grad: float32 [1024, 24], P(('fsdp', 'ctx'), 'tp')
- state_proj_grad: float32 [1024, 256], P(('fsdp', 'ctx'))
- keyval_grad: float32 [1024, 256], P(('fsdp', 'ctx'))
- query_grad: float32 [1024, 512], P(('fsdp', 'ctx'), 'tp')
- step_bias_grad: float32 [24], P('tp')
- decay_log_grad: float32 [24], P('tp')
- skip_gain_grad: float32 [24], P('tp')
- mixer_out_grad: float32 [1536, 1024], P('tp', ('fsdp', 'ctx'))
- attn_out_grad: float32 [512, 1024], P('tp', ('fsdp', 'ctx'))
- gate_grad: float32 [1024, 2048], P(('fsdp', 'ctx'), 'tp')
- up_grad: float32 [1024, 2048], P(('fsdp', 'ctx'), 'tp')
- down_grad: float32 [2048, 1024], P('tp', ('fsdp', 'ctx'))
Inputs may be any that keep to these rules, and one draw needn't show every extreme that they name: `lengths`: each sequence's live positions; in every draw one sequence has all 1024 live.
All inputs are finite; a program needn't handle non-finite values.
Results may differ from a plain program's by a relative error of at most 0.035.
Values may be sent and summed in bfloat16 or wider, within the bound.
A program may use at most 128 MiB of HBM per device.

v0:
```python
import jax
import jax.numpy as jnp
from jax import lax
from jax.sharding import PartitionSpec as P

MDIM = 64
STATE = 128
QHEADS = 8
KVHEADS = 2
HDIM = 64
STRETCH = 256


EPS = 1e-05
ROPE_BASE = 10000.0
NEG_FILL = -1e30
exact_dots = lax.Precision.HIGHEST


def carried_in(shard, axis, join, neutral, backward):
    count = lax.axis_size(axis)
    place = lax.axis_index(axis)
    ahead = count - 1 - place if backward else place
    gathered = jax.tree.map(
        lambda a, kind: lax.all_gather(a.astype(kind), axis), shard, (jnp.bfloat16, jnp.bfloat16)
    )
    state = jax.tree.map(lambda a, e: jnp.zeros_like(a) + jnp.asarray(e, a.dtype), shard, neutral)

    def one(turn, state):
        source = count - 1 - turn if backward else turn
        return join(
            state,
            jax.tree.map(
                lambda a, own: lax.dynamic_index_in_dim(a, source, 0, False).astype(own.dtype),
                gathered,
                shard,
            ),
        )

    return lax.fori_loop(0, ahead, one, state)


def angle_tables(places, width):
    half_width = width // 2
    frequencies = ROPE_BASE ** (-(jnp.arange(half_width).astype(jnp.float32) * 2.0 / width))
    angles = places.astype(jnp.float32)[:, None] * frequencies[None, :]
    return (jnp.cos(angles)[:, None, :], jnp.sin(angles)[:, None, :], half_width)


def rotate(vectors, places):
    cosine, sine_part, half_width = angle_tables(places, vectors.shape[-1])
    first_half = vectors[..., :half_width]
    second = vectors[..., half_width:]
    return jnp.concatenate(
        [first_half * cosine - second * sine_part, second * cosine + first_half * sine_part],
        axis=-1,
    )


def rotate_back(grad_rows, places):
    cosine, sine_part, half_width = angle_tables(places, grad_rows.shape[-1])
    first_half = grad_rows[..., :half_width]
    second = grad_rows[..., half_width:]
    return jnp.concatenate(
        [first_half * cosine + second * sine_part, second * cosine - first_half * sine_part],
        axis=-1,
    )


def step_decay(step_raw, inputs, step_bias, decay_log, live_mask):
    step_size = jax.nn.softplus(step_raw + step_bias[None, :]) * live_mask[:, None]
    log_decay = -jnp.exp(decay_log)[None, :] * step_size
    driven = inputs * step_size[:, :, None]
    return (log_decay, driven)


def state_space(
    inputs, gate_pre, b_proj, c_proj, step_raw, step_bias, decay_log, skip_gain, live_mask, state_in
):
    row_count, head_count, head_width = inputs.shape
    log_decay, driven = step_decay(step_raw, inputs, step_bias, decay_log, live_mask)
    block_count = row_count // STRETCH
    lower = jnp.arange(STRETCH)[:, None] >= jnp.arange(STRETCH)[None, :]

    def advance(state, pieces):
        decay_part, driven_part, b_part, c_part, input_part = pieces
        cumulative = jnp.cumsum(decay_part, axis=0)
        differences = cumulative[:, None, :] - cumulative[None, :, :]
        decays = jnp.exp(jnp.where(lower[:, :, None], differences, NEG_FILL))
        products = jnp.dot(c_part, b_part.T, precision=exact_dots)
        within = jnp.einsum("ts,tsh,shp->thp", products, decays, driven_part, precision=exact_dots)
        carried = (
            jnp.einsum("tn,hnp->thp", c_part, state, precision=exact_dots)
            * jnp.exp(cumulative)[:, :, None]
        )
        tail_decay = jnp.exp(cumulative[-1][None, :] - cumulative)
        new_state = jnp.exp(cumulative[-1])[:, None, None] * state + jnp.einsum(
            "sh,sn,shp->hnp", tail_decay, b_part, driven_part, precision=exact_dots
        )
        return (new_state, within + carried + skip_gain[None, :, None] * input_part)

    state_out, outputs = lax.scan(
        advance,
        state_in,
        (
            log_decay.reshape(block_count, STRETCH, head_count),
            driven.reshape(block_count, STRETCH, head_count, head_width),
            b_proj.reshape(block_count, STRETCH, -1),
            c_proj.reshape(block_count, STRETCH, -1),
            inputs.reshape(block_count, STRETCH, head_count, head_width),
        ),
    )
    mixer_y = outputs.reshape(row_count, head_count, head_width)
    return (mixer_y * jax.nn.silu(gate_pre), state_out)


def chain_states(earlier, later):
    return (earlier[0] * later[0], later[0][:, None, None] * earlier[1] + later[1])


def per_device(
    tokens,
    lengths,
    cotangent,
    in_norm_gain,
    ffn_norm_gain,
    mixer_in,
    step_weight,
    state_proj,
    keyval_weight,
    query_weight,
    step_bias,
    decay_log,
    skip_gain,
    mixer_out,
    attn_out,
    ffn_gate,
    ffn_up,
    ffn_down,
):
    (
        gain_in,
        gain_ffn,
        full_mixer_in,
        full_step,
        full_state,
        full_keyval,
        full_query,
        full_mixer_out,
        full_attn_out,
        full_gate,
        full_up,
        full_down,
    ) = (
        lax.all_gather(in_norm_gain, ("fsdp", "ctx"), axis=0, tiled=True),
        lax.all_gather(ffn_norm_gain, ("fsdp", "ctx"), axis=0, tiled=True),
        lax.all_gather(mixer_in, ("fsdp", "ctx"), axis=0, tiled=True),
        lax.all_gather(step_weight, ("fsdp", "ctx"), axis=0, tiled=True),
        lax.all_gather(state_proj, ("fsdp", "ctx"), axis=0, tiled=True),
        lax.all_gather(keyval_weight, ("fsdp", "ctx"), axis=0, tiled=True),
        lax.all_gather(query_weight, ("fsdp", "ctx"), axis=0, tiled=True),
        lax.all_gather(mixer_out, ("fsdp", "ctx"), axis=1, tiled=True),
        lax.all_gather(attn_out, ("fsdp", "ctx"), axis=1, tiled=True),
        lax.all_gather(ffn_gate, ("fsdp", "ctx"), axis=0, tiled=True),
        lax.all_gather(ffn_up, ("fsdp", "ctx"), axis=0, tiled=True),
        lax.all_gather(ffn_down, ("fsdp", "ctx"), axis=1, tiled=True),
    )
    width_model = full_gate.shape[0]
    row_count = tokens.shape[1]
    heads_here = step_weight.shape[1]
    inner_here = heads_here * MDIM
    query_here = query_weight.shape[1] // HDIM
    kv_span = KVHEADS * HDIM
    ctx_index = lax.axis_index("ctx")
    tp_index = lax.axis_index("tp")
    places = ctx_index * row_count + jnp.arange(row_count, dtype=jnp.int32)
    length = lengths[0]
    live_mask = (places < length).astype(jnp.float32)
    inputs_f = tokens[0].astype(jnp.float32)
    inv_one = lax.rsqrt(jnp.mean(inputs_f * inputs_f, axis=-1, keepdims=True) + EPS)
    normed = (inputs_f * inv_one * gain_in.astype(jnp.float32)).astype(jnp.bfloat16)
    mixer_flat = full_mixer_in.reshape(width_model, -1)
    projected = jnp.dot(normed, mixer_flat, preferred_element_type=jnp.float32).reshape(
        row_count, 2, heads_here, MDIM
    )
    gate_pre = projected[:, 0]
    inputs = projected[:, 1]
    step_raw = jnp.dot(normed, full_step, preferred_element_type=jnp.float32)
    state_cols = jnp.dot(normed, full_state, preferred_element_type=jnp.float32)
    b_proj = state_cols[:, :STATE]
    c_proj = state_cols[:, STATE:]
    keyval_cols = jnp.dot(normed, full_keyval, preferred_element_type=jnp.float32)
    kv_head = tp_index * query_here // (QHEADS // KVHEADS)
    key_raw = lax.dynamic_slice_in_dim(keyval_cols, kv_head * HDIM, HDIM, 1)
    value_raw = lax.dynamic_slice_in_dim(keyval_cols, kv_span + kv_head * HDIM, HDIM, 1)
    queries = jnp.dot(normed, full_query, preferred_element_type=jnp.float32).reshape(
        row_count, query_here, HDIM
    )
    query_b = rotate(queries, places).astype(jnp.bfloat16)
    key_b = rotate(key_raw[:, None, :], places)[:, 0].astype(jnp.bfloat16)
    own_keyval = jnp.concatenate([key_b, value_raw.astype(jnp.bfloat16)], axis=1)
    all_keyval = lax.all_gather(own_keyval, "ctx", axis=0, tiled=True)
    all_keys = all_keyval[:, :HDIM]
    values = all_keyval[:, HDIM:]
    log_decay, driven = step_decay(step_raw, inputs, step_bias, decay_log, live_mask)
    cumulative = jnp.cumsum(log_decay, axis=0)
    own_decay = jnp.exp(cumulative[-1])
    own_state = jnp.einsum(
        "sh,sn,shp->hnp",
        jnp.exp(cumulative[-1][None, :] - cumulative),
        b_proj,
        driven,
        precision=exact_dots,
    )
    identity = (jnp.ones_like(own_decay), jnp.zeros_like(own_state))
    decay_before, state_in = carried_in(
        (own_decay, own_state), "ctx", chain_states, identity, False
    )

    def mixer_fn(
        input_part,
        gate_part,
        b_part,
        c_part,
        step_part,
        bias_part,
        decay_part,
        skip_part,
        state_part,
    ):
        return state_space(
            input_part,
            gate_part,
            b_part,
            c_part,
            step_part,
            bias_part,
            decay_part,
            skip_part,
            live_mask,
            state_part,
        )

    (gated, state_end), mixer_back = jax.vjp(
        mixer_fn,
        inputs,
        gate_pre,
        b_proj,
        c_proj,
        step_raw,
        step_bias,
        decay_log,
        skip_gain,
        state_in,
    )
    gated_b = gated.astype(jnp.bfloat16).reshape(row_count, inner_here)
    block_rows = min(512, row_count)
    score_scale = HDIM ** (-0.5)
    block_count = (ctx_index + 1) * (row_count // block_rows)

    def key_block(block_index):
        start = block_index * block_rows
        key_part = lax.dynamic_slice_in_dim(all_keys, start, block_rows, 0)
        value_part = lax.dynamic_slice_in_dim(values, start, block_rows, 0)
        scores = (
            jnp.einsum("qhd,kd->hqk", query_b, key_part, preferred_element_type=jnp.float32)
            * score_scale
        )
        key_places = start + jnp.arange(block_rows, dtype=jnp.int32)
        allowed = (key_places[None, :] <= places[:, None]) & (key_places[None, :] < length)
        return (jnp.where(allowed[None], scores, NEG_FILL), key_part, value_part)

    def running_total(block_index, loop_state):
        peak_score, mass_total = loop_state
        scores, key_part, value_part = key_block(block_index)
        new_peak = jnp.maximum(peak_score, jnp.max(scores, axis=-1))
        mass_total = mass_total * jnp.exp(peak_score - new_peak) + jnp.sum(
            jnp.exp(scores - new_peak[..., None]), axis=-1
        )
        return (new_peak, mass_total)

    peak_score, mass_total = lax.fori_loop(
        0,
        block_count,
        running_total,
        (
            jnp.full((query_here, row_count), NEG_FILL, jnp.float32),
            jnp.zeros((query_here, row_count), jnp.float32),
        ),
    )
    log_total = peak_score + jnp.log(mass_total)

    def weighted_sum(block_index, summed):
        scores, key_part, value_part = key_block(block_index)
        prob_b = jnp.exp(scores - log_total[..., None]).astype(jnp.bfloat16)
        return summed + jnp.einsum(
            "hqk,kd->qhd", prob_b, value_part, preferred_element_type=jnp.float32
        )

    attended_b = lax.fori_loop(
        0, block_count, weighted_sum, jnp.zeros((row_count, query_here, HDIM), jnp.float32)
    ).astype(jnp.bfloat16)
    attn_flat_b = attended_b.reshape(row_count, query_here * HDIM)
    partial_term = jnp.dot(gated_b, full_mixer_out, preferred_element_type=jnp.float32) + jnp.dot(
        attn_flat_b, full_attn_out, preferred_element_type=jnp.float32
    )
    mixed = lax.psum(partial_term.astype(jnp.bfloat16), "tp").astype(jnp.float32)
    resid = inputs_f + mixed
    inv_two = lax.rsqrt(jnp.mean(resid * resid, axis=-1, keepdims=True) + EPS)
    normed_two = (resid * inv_two * gain_ffn.astype(jnp.float32)).astype(jnp.bfloat16)
    gate_val = jnp.dot(normed_two, full_gate, preferred_element_type=jnp.float32)
    up_val = jnp.dot(normed_two, full_up, preferred_element_type=jnp.float32)
    act_b = (jax.nn.silu(gate_val) * up_val).astype(jnp.bfloat16)
    ffn_total = lax.psum(
        jnp.dot(act_b, full_down, preferred_element_type=jnp.float32).astype(jnp.bfloat16), "tp"
    ).astype(jnp.float32)
    block_out = (resid + ffn_total).astype(jnp.bfloat16)
    (
        gain_in,
        gain_ffn,
        full_mixer_in,
        full_step,
        full_state,
        full_keyval,
        full_query,
        full_mixer_out,
        full_attn_out,
        full_gate,
        full_up,
        full_down,
    ) = (
        lax.all_gather(in_norm_gain, ("fsdp", "ctx"), axis=0, tiled=True),
        lax.all_gather(ffn_norm_gain, ("fsdp", "ctx"), axis=0, tiled=True),
        lax.all_gather(mixer_in, ("fsdp", "ctx"), axis=0, tiled=True),
        lax.all_gather(step_weight, ("fsdp", "ctx"), axis=0, tiled=True),
        lax.all_gather(state_proj, ("fsdp", "ctx"), axis=0, tiled=True),
        lax.all_gather(keyval_weight, ("fsdp", "ctx"), axis=0, tiled=True),
        lax.all_gather(query_weight, ("fsdp", "ctx"), axis=0, tiled=True),
        lax.all_gather(mixer_out, ("fsdp", "ctx"), axis=1, tiled=True),
        lax.all_gather(attn_out, ("fsdp", "ctx"), axis=1, tiled=True),
        lax.all_gather(ffn_gate, ("fsdp", "ctx"), axis=0, tiled=True),
        lax.all_gather(ffn_up, ("fsdp", "ctx"), axis=0, tiled=True),
        lax.all_gather(ffn_down, ("fsdp", "ctx"), axis=1, tiled=True),
    )
    cot_rows = cotangent[0]
    act_grad = jnp.dot(cot_rows, full_down.T, preferred_element_type=jnp.float32)
    sigmoid_gate = jax.nn.sigmoid(gate_val)
    dgate_b = (act_grad * up_val * sigmoid_gate * (1.0 + gate_val * (1.0 - sigmoid_gate))).astype(
        jnp.bfloat16
    )
    dup_b = (act_grad * gate_val * sigmoid_gate).astype(jnp.bfloat16)
    down_grad = jnp.dot(act_b.T, cot_rows, preferred_element_type=jnp.float32)
    gate_grad = jnp.dot(normed_two.T, dgate_b, preferred_element_type=jnp.float32)
    up_grad = jnp.dot(normed_two.T, dup_b, preferred_element_type=jnp.float32)
    dnormed_two = lax.psum(
        (
            jnp.dot(dgate_b, full_gate.T, preferred_element_type=jnp.float32)
            + jnp.dot(dup_b, full_up.T, preferred_element_type=jnp.float32)
        ).astype(jnp.bfloat16),
        "tp",
    ).astype(jnp.float32)
    scaled_two = gain_ffn.astype(jnp.float32) * dnormed_two
    ffn_norm_grad = jnp.sum(dnormed_two * resid * inv_two, axis=0)
    dresid = (
        cot_rows.astype(jnp.float32)
        + inv_two * scaled_two
        - resid * inv_two**3 * jnp.mean(scaled_two * resid, axis=-1, keepdims=True)
    )
    dmixed_b = dresid.astype(jnp.bfloat16)
    mixer_out_grad = jnp.dot(gated_b.T, dmixed_b, preferred_element_type=jnp.float32)
    attn_out_grad = jnp.dot(attn_flat_b.T, dmixed_b, preferred_element_type=jnp.float32)
    dgated = jnp.dot(dmixed_b, full_mixer_out.T, preferred_element_type=jnp.float32).reshape(
        row_count, heads_here, MDIM
    )
    dattended_b = (
        jnp.dot(dmixed_b, full_attn_out.T, preferred_element_type=jnp.float32)
        .reshape(row_count, query_here, HDIM)
        .astype(jnp.bfloat16)
    )
    dstate_direct = jnp.einsum(
        "sn,sh,shp->hnp",
        c_proj,
        jnp.exp(cumulative),
        dgated * jax.nn.silu(gate_pre),
        precision=exact_dots,
    )
    decay_after, later_grad = carried_in(
        (own_decay, dstate_direct), "ctx", chain_states, identity, True
    )
    dinputs, dgate_pre, db_proj, dc_proj, dstep_raw, dbias, ddecay, dskip, dstate_unused = (
        mixer_back((dgated, later_grad))
    )
    row_terms = jnp.sum(dattended_b.astype(jnp.float32) * attended_b.astype(jnp.float32), axis=-1).T

    def back_block(block_index, loop_state):
        dquery, dkeyval = loop_state
        scores, key_part, value_part = key_block(block_index)
        prob_rows = jnp.exp(scores - log_total[..., None])
        dprob = jnp.einsum(
            "qhd,kd->hqk", dattended_b, value_part, preferred_element_type=jnp.float32
        )
        dscore_b = (prob_rows * (dprob - row_terms[..., None])).astype(jnp.bfloat16)
        dquery = (
            dquery
            + jnp.einsum("hqk,kd->qhd", dscore_b, key_part, preferred_element_type=jnp.float32)
            * score_scale
        )
        dkey_part = (
            jnp.einsum("hqk,qhd->kd", dscore_b, query_b, preferred_element_type=jnp.float32)
            * score_scale
        )
        dvalue_part = jnp.einsum(
            "hqk,qhd->kd",
            prob_rows.astype(jnp.bfloat16),
            dattended_b,
            preferred_element_type=jnp.float32,
        )
        dkeyval = lax.dynamic_update_slice_in_dim(
            dkeyval, jnp.concatenate([dkey_part, dvalue_part], axis=1), block_index * block_rows, 0
        )
        return (dquery, dkeyval)

    dquery, dkeyval = lax.fori_loop(
        0,
        block_count,
        back_block,
        (
            jnp.zeros((row_count, query_here, HDIM), jnp.float32),
            jnp.zeros((all_keyval.shape[0], 2 * HDIM), jnp.float32),
        ),
    )
    own_dkeyval = lax.psum_scatter(
        dkeyval.astype(jnp.bfloat16), "ctx", scatter_dimension=0, tiled=True
    ).astype(jnp.float32)
    dkey_rot = rotate_back(own_dkeyval[:, None, :HDIM], places)[:, 0]
    dkeyval_full = jnp.zeros((row_count, 2 * kv_span), jnp.float32)
    dkeyval_full = lax.dynamic_update_slice_in_dim(dkeyval_full, dkey_rot, kv_head * HDIM, 1)
    dkeyval_full = lax.dynamic_update_slice_in_dim(
        dkeyval_full, own_dkeyval[:, HDIM:], kv_span + kv_head * HDIM, 1
    )
    dkeyval_b = dkeyval_full.astype(jnp.bfloat16)
    dquery_b = (
        rotate_back(dquery, places).reshape(row_count, query_here * HDIM).astype(jnp.bfloat16)
    )
    dstate_b = jnp.concatenate([db_proj, dc_proj], axis=1).astype(jnp.bfloat16)
    dmix_in_b = (
        jnp.stack([dgate_pre, dinputs], axis=1)
        .reshape(row_count, 2 * inner_here)
        .astype(jnp.bfloat16)
    )
    dstep_b = dstep_raw.astype(jnp.bfloat16)
    mixer_in_grad = jnp.dot(normed.T, dmix_in_b, preferred_element_type=jnp.float32).reshape(
        width_model, 2, inner_here
    )
    step_grad = jnp.dot(normed.T, dstep_b, preferred_element_type=jnp.float32)
    state_grad = jnp.dot(normed.T, dstate_b, preferred_element_type=jnp.float32)
    keyval_grad = jnp.dot(normed.T, dkeyval_b, preferred_element_type=jnp.float32)
    query_grad = jnp.dot(normed.T, dquery_b, preferred_element_type=jnp.float32)
    back_flat = full_mixer_in.reshape(width_model, -1)
    group_term = jnp.dot(dmix_in_b, back_flat.T, preferred_element_type=jnp.float32)
    group_term = group_term + jnp.dot(dstep_b, full_step.T, preferred_element_type=jnp.float32)
    group_term = group_term + jnp.dot(dstate_b, full_state.T, preferred_element_type=jnp.float32)
    group_term = group_term + jnp.dot(dkeyval_b, full_keyval.T, preferred_element_type=jnp.float32)
    group_term = group_term + jnp.dot(dquery_b, full_query.T, preferred_element_type=jnp.float32)
    dnormed = lax.psum(group_term.astype(jnp.bfloat16), "tp").astype(jnp.float32)
    scaled_one = gain_in.astype(jnp.float32) * dnormed
    in_norm_grad = jnp.sum(dnormed * inputs_f * inv_one, axis=0)
    input_grad = (
        dresid
        + inv_one * scaled_one
        - inputs_f * inv_one**3 * jnp.mean(scaled_one * inputs_f, axis=-1, keepdims=True)
    )
    state_grad, keyval_grad = (
        lax.psum(state_grad.astype(jnp.bfloat16), "tp").astype(jnp.float32),
        lax.psum(keyval_grad.astype(jnp.bfloat16), "tp").astype(jnp.float32),
    )
    (
        in_norm_rows,
        ffn_norm_rows,
        mixer_in_rows,
        step_rows,
        state_rows,
        keyval_rows,
        query_rows,
        mixer_out_rows,
        attn_out_rows,
        gate_rows,
        up_rows,
        down_rows,
    ) = (
        lax.psum_scatter(in_norm_grad, ("fsdp", "ctx"), scatter_dimension=0, tiled=True),
        lax.psum_scatter(ffn_norm_grad, ("fsdp", "ctx"), scatter_dimension=0, tiled=True),
        lax.psum_scatter(mixer_in_grad, ("fsdp", "ctx"), scatter_dimension=0, tiled=True),
        lax.psum_scatter(step_grad, ("fsdp", "ctx"), scatter_dimension=0, tiled=True),
        lax.psum_scatter(state_grad, ("fsdp", "ctx"), scatter_dimension=0, tiled=True),
        lax.psum_scatter(keyval_grad, ("fsdp", "ctx"), scatter_dimension=0, tiled=True),
        lax.psum_scatter(query_grad, ("fsdp", "ctx"), scatter_dimension=0, tiled=True),
        lax.psum_scatter(mixer_out_grad, ("fsdp", "ctx"), scatter_dimension=1, tiled=True),
        lax.psum_scatter(attn_out_grad, ("fsdp", "ctx"), scatter_dimension=1, tiled=True),
        lax.psum_scatter(gate_grad, ("fsdp", "ctx"), scatter_dimension=0, tiled=True),
        lax.psum_scatter(up_grad, ("fsdp", "ctx"), scatter_dimension=0, tiled=True),
        lax.psum_scatter(down_grad, ("fsdp", "ctx"), scatter_dimension=1, tiled=True),
    )
    bias_grad, decay_grad, skip_grad = lax.psum((dbias, ddecay, dskip), ("fsdp", "ctx"))
    return (
        block_out[None],
        input_grad[None],
        in_norm_rows,
        ffn_norm_rows,
        mixer_in_rows,
        step_rows,
        state_rows,
        keyval_rows,
        query_rows,
        bias_grad,
        decay_grad,
        skip_grad,
        mixer_out_rows,
        attn_out_rows,
        gate_rows,
        up_rows,
        down_rows,
    )


def solution(mesh):
    placed = (
        P("fsdp", "ctx", None),
        P("fsdp"),
        P("fsdp", "ctx", None),
        P(("fsdp", "ctx")),
        P(("fsdp", "ctx")),
        P(("fsdp", "ctx"), None, "tp"),
        P(("fsdp", "ctx"), "tp"),
        P(("fsdp", "ctx"), None),
        P(("fsdp", "ctx"), None),
        P(("fsdp", "ctx"), "tp"),
        P("tp"),
        P("tp"),
        P("tp"),
        P("tp", ("fsdp", "ctx")),
        P("tp", ("fsdp", "ctx")),
        P(("fsdp", "ctx"), "tp"),
        P(("fsdp", "ctx"), "tp"),
        P("tp", ("fsdp", "ctx")),
    )
    return jax.shard_map(
        per_device,
        mesh=mesh,
        in_specs=placed,
        out_specs=(
            P("fsdp", "ctx", None),
            P("fsdp", "ctx", None),
            P(("fsdp", "ctx")),
            P(("fsdp", "ctx")),
            P(("fsdp", "ctx"), None, "tp"),
            P(("fsdp", "ctx"), "tp"),
            P(("fsdp", "ctx"), None),
            P(("fsdp", "ctx"), None),
            P(("fsdp", "ctx"), "tp"),
            P("tp"),
            P("tp"),
            P("tp"),
            P("tp", ("fsdp", "ctx")),
            P("tp", ("fsdp", "ctx")),
            P(("fsdp", "ctx"), "tp"),
            P(("fsdp", "ctx"), "tp"),
            P("tp", ("fsdp", "ctx")),
        ),
        check_vma=False,
    )
```

profile of v0, /device:TPU:0, one launch (start us, length us, event | category | flops | bytes accessed | tf_op | source)
XLA Modules:
  0.0 1431.3 jit_solution(4830759058994456628)
XLA Ops:
  10.1 22.3 %all-gather.2 = bf16[8,1,128]{2,1,0:T(2,128)(2,1)S(1)} all-gather(bf16[1,1,128]{2,1,0:T(2,128)(2,1)} %bitcast.875), channel_id=1, replica_groups=mesh['fsdp'=4,'ctx'=2,'tp'=4] {'fsdp','ctx'}, dimensions={0}, use_global_device_ids=true | all-gather | bytes 2304 | tf_op jit(solution)/shard_map/all_gather | solution.py:155
  33.8 26.4 %all_gather.70 = bf16[1024,6]{0,1:T(8,128)(2,1)S(1)} all-gather(bf16[128,6]{0,1:T(8,128)(2,1)} %param.38), channel_id=1, replica_groups=mesh['fsdp'=4,'ctx'=2,'tp'=4] {'fsdp','ctx'}, dimensions={0}, use_global_device_ids=true | all-gather | bytes 13824 | tf_op jit(solution)/shard_map/all_gather | solution.py:158
  60.1 31.4 %all_gather.77 = bf16[1024,256]{1,0:T(8,128)(2,1)S(1)} all-gather(bf16[128,256]{1,0:T(8,128)(2,1)} %param.40), channel_id=1, replica_groups=mesh['fsdp'=4,'ctx'=2,'tp'=4] {'fsdp','ctx'}, dimensions={0}, use_global_device_ids=true | all-gather | bytes 589824 | tf_op jit(solution)/shard_map/all_gather | solution.py:160
  100.3 30.8 %all_gather.79 = bf16[1024,128]{1,0:T(8,128)(2,1)S(1)} all-gather(bf16[128,128]{1,0:T(8,128)(2,1)S(1)} %copy-done.93), channel_id=1, replica_groups=mesh['fsdp'=4,'ctx'=2,'tp'=4] {'fsdp','ctx'}, dimensions={0}, use_global_device_ids=true | all-gather | bytes 294912 | tf_op jit(solution)/shard_map/all_gather | solution.py:161
  143.6 26.4 %all_gather.80 = bf16[128,1024]{1,0:T(8,128)(2,1)S(1)} all-gather(bf16[128,128]{1,0:T(8,128)(2,1)S(1)} %copy-done.94), channel_id=1, replica_groups=mesh['fsdp'=4,'ctx'=2,'tp'=4] {'fsdp','ctx'}, dimensions={1}, use_global_device_ids=true | all-gather | bytes 294912 | tf_op jit(solution)/shard_map/all_gather | solution.py:163
  170.8 31.4 %all_gather.73 = bf16[1024,256]{1,0:T(8,128)(2,1)S(1)} all-gather(bf16[128,256]{1,0:T(8,128)(2,1)S(1)} %copy-done.80), channel_id=1, replica_groups=mesh['fsdp'=4,'ctx'=2,'tp'=4] {'fsdp','ctx'}, dimensions={0}, use_global_device_ids=true | all-gather | bytes 589824 | tf_op jit(solution)/shard_map/all_gather | solution.py:159
  205.3 28.7 %all_gather.76 = bf16[384,1024]{1,0:T(8,128)(2,1)} all-gather(bf16[384,128]{1,0:T(8,128)(2,1)S(1)} %copy-done.78), channel_id=1, replica_groups=mesh['fsdp'=4,'ctx'=2,'tp'=4] {'fsdp','ctx'}, dimensions={1}, use_global_device_ids=true | all-gather | bytes 884736 | tf_op jit(solution)/shard_map/all_gather | solution.py:162
  254.6 54.5 %while.134 = (s32[]{:T(128)}, f32[6,128,64]{1,2,0:T(8,128)S(1)}, f32[2,256,6,64]{1,0,3,2:T(2,128)}, f32[2,256,256,6]{2,1,3,0:T(8,128)}, f32[2,128,256]{1,2,0:T(8...) while((s32[]{:T(128)}, f32[6,128,64]{1,2,0:T(8,128)S(1)}, ...), condition=%wide.region_8.9_spmd.clone.clone, body=%wide.region_5.8_spmd.clone.clone.sunk | while | flops 708675072 | bytes 16335581 | solution.py:102
  263.2 8.9 dynamic_update_slice.205
  315.6 17.1 %all-gather.4 = bf16[8,1,128]{2,1,0:T(2,128)(2,1)S(1)} all-gather(bf16[1,1,128]{2,1,0:T(2,128)(2,1)S(1)} %bitcast.876), channel_id=1, replica_groups=mesh['fsdp'=4,'ctx'=2,'tp'=4] {'fsdp','ctx'}, dimensions={0}, use_global_device_ids=true | all-gather | bytes 2304 | tf_op jit(solution)/shard_map/all_gather | solution.py:156
  332.7 15.6 %all-reduce.10.cloned.1.call-done = bf16[512,1024]{1,0:T(8,128)(2,1)} async-done(((bf16[512,1024]{1,0:T(8,128)(2,1)}), bf16[512,1024]{1,0:T(8,128)(2,1)}) %all-reduce.10.cloned.1.call-update) | async-done | bytes 1048592 | tf_op jit(solution)/shard_map/psum | solution.py:307
  351.5 39.8 %all-gather.12.cloned.1.call-done = bf16[1024,512]{1,0:T(8,128)(2,1)} async-done(((bf16[128,512]{1,0:T(8,128)(2,1)}), bf16[1024,512]{1,0:T(8,128)(2,1)}) %all-gather.12.cloned.1.call-update) | async-done | bytes 1048592 | tf_op jit(solution)/shard_map/all_gather | solution.py:164
  394.5 37.9 %all-gather.14.cloned.1.call-done = bf16[1024,512]{1,0:T(8,128)(2,1)} async-done(((bf16[128,512]{1,0:T(8,128)(2,1)}), bf16[1024,512]{1,0:T(8,128)(2,1)}) %all-gather.14.cloned.1.call-update) | async-done | bytes 1048592 | tf_op jit(solution)/shard_map/all_gather | solution.py:165
  435.6 37.2 %all-gather.16.cloned.1.call-done = bf16[512,1024]{1,0:T(8,128)(2,1)} async-done(((bf16[512,128]{1,0:T(8,128)(2,1)}), bf16[512,1024]{1,0:T(8,128)(2,1)}) %all-gather.16.cloned.1.call-update) | async-done | bytes 1048592 | tf_op jit(solution)/shard_map/all_gather | solution.py:166
  489.1 26.4 %all-reduce.12.cloned.1.call-done = bf16[512,1024]{1,0:T(8,128)(2,1)} async-done(((bf16[512,1024]{1,0:T(8,128)(2,1)}), bf16[512,1024]{1,0:T(8,128)(2,1)}) %all-reduce.12.cloned.1.call-update) | async-done | bytes 1048592 | tf_op jit(solution)/shard_map/psum | solution.py:355
  538.2 95.2 %while.135 = (s32[]{:T(128)}, f32[6]{0:T(128)}, f32[6,128,64]{1,2,0:T(8,128)S(1)}, f32[2,256,6]{1,2,0:T(8,128)}, f32[2,256,6,64]{1,0,3,2:T(2,128)}, /*index=5*/b...) while((s32[]{:T(128)}, f32[6]{0:T(128)}, ...), condition=%wide.region_31.32_spmd.clone, body=%wide.region_22.31_spmd.clone.sunk | while | flops 1413523968 | bytes 16896452 | solution.py:102
  544.0 9.0 dynamic_update_slice.210
  576.3 9.0 dynamic_update_slice.211
  591.5 9.0 dynamic_update_slice.210
  623.8 9.0 dynamic_update_slice.211
  688.6 53.9 %all-reduce.14.cloned.1.call-done = (bf16[512,1024]{1,0:T(8,128)(2,1)}, bf16[512,1024]{1,0:T(8,128)(2,1)}, bf16[1024,256]{1,0:T(8,128)(2,1)}, bf16[1024,256]{1,0:T(8,128)(2,1)}) async-done(((bf16[512,1024]{1,0:T(8,128)(2,1)}, bf16[512,1024]{1,0:T(8,128)(2,1)}, bf16[1024,256]{1,0:T(8,128)(2,1)}, bf16[1024,256]{1,0:T(8,128)(2,1)}), (bf16[512,1024]{1,0:T(8,128)(2,1)}, bf16[512,1024]{1,0:T(8,128)(2,1)}, ...) | async-done | bytes 3145744 | tf_op jit(solution)/shard_map/psum | solution.py:314
  750.4 23.5 %all-reduce.4 = (f32[1024]{0:T(1024)S(1)}, f32[1024]{0:T(1024)S(1)}, f32[6]{0:T(128)}, f32[6]{0:T(128)}, f32[6]{0:T(128)}) all-reduce(f32[1024]{0:T(1024)S(1)} %get-tuple-element.1708, f32[1024]{0:T(1024)S(1)} %copy-done.106, f32[6]{0:T(128)S(1)} %copy-done.114, ...), channel_id=5, replica_groups=mesh['fsdp'=4,'ctx'=2,'tp'=4] {'fsdp','ctx'}, use_global_device_ids=true, to_apply=%region_40.41.clone | all-reduce | flops 2066 | bytes 16528
  779.3 42.7 %reduce-scatter.14.cloned.1.call-done = f32[128,2,384]{2,0,1:T(8,128)} async-done(((f32[1024,2,384]{2,0,1:T(8,128)}), f32[128,2,384]{2,0,1:T(8,128)}) %reduce-scatter.14.cloned.1.call-update) | async-done | bytes 393232 | tf_op jit(solution)/shard_map/reduce_scatter | solution.py:493
  824.0 54.4 %reduce-scatter.16.cloned.1.call-done = f32[128,6]{0,1:T(8,128)} async-done(((f32[1024,6]{0,1:T(8,128)}), f32[128,6]{0,1:T(8,128)}) %reduce-scatter.16.cloned.1.call-update) | async-done | bytes 3088 | tf_op jit(solution)/shard_map/reduce_scatter | solution.py:494
  878.4 65.8 %reduce-scatter.26.cloned.1.call-done = f32[128,128]{1,0:T(8,128)} async-done(((f32[128,1024]{1,0:T(8,128)}), f32[128,128]{1,0:T(8,128)}) %reduce-scatter.26.cloned.1.call-update) | async-done | bytes 65552 | tf_op jit(solution)/shard_map/reduce_scatter | solution.py:499
  944.2 64.7 %reduce-scatter.22.cloned.1.call-done = f32[128,128]{1,0:T(8,128)} async-done(((f32[1024,128]{1,0:T(8,128)}), f32[128,128]{1,0:T(8,128)}) %reduce-scatter.22.cloned.1.call-update) | async-done | bytes 65552 | tf_op jit(solution)/shard_map/reduce_scatter | solution.py:497
  1008.9 69.1 %reduce-scatter.24.cloned.1.call-done = f32[384,128]{1,0:T(8,128)} async-done(((f32[384,1024]{1,0:T(8,128)}), f32[384,128]{1,0:T(8,128)}) %reduce-scatter.24.cloned.1.call-update) | async-done | bytes 196624 | tf_op jit(solution)/shard_map/reduce_scatter | solution.py:498
  1078.1 70.8 %reduce-scatter.28.cloned.1.call-done = f32[128,512]{1,0:T(8,128)} async-done(((f32[1024,512]{1,0:T(8,128)}), f32[128,512]{1,0:T(8,128)}) %reduce-scatter.28.cloned.1.call-update) | async-done | bytes 262160 | tf_op jit(solution)/shard_map/reduce_scatter | solution.py:500
  1148.9 70.8 %reduce-scatter.30.cloned.1.call-done = f32[128,512]{1,0:T(8,128)} async-done(((f32[1024,512]{1,0:T(8,128)}), f32[128,512]{1,0:T(8,128)}) %reduce-scatter.30.cloned.1.call-update) | async-done | bytes 262160 | tf_op jit(solution)/shard_map/reduce_scatter | solution.py:501
  1219.7 71.3 %reduce-scatter.32.cloned.1.call-done = f32[512,128]{1,0:T(8,128)} async-done(((f32[512,1024]{1,0:T(8,128)}), f32[512,128]{1,0:T(8,128)}) %reduce-scatter.32.cloned.1.call-update) | async-done | bytes 262160 | tf_op jit(solution)/shard_map/reduce_scatter | solution.py:502
  1290.9 66.3 %reduce-scatter.18.cloned.1.call-done = f32[128,256]{1,0:T(8,128)} async-done(((f32[1024,256]{1,0:T(8,128)}), f32[128,256]{1,0:T(8,128)}) %reduce-scatter.18.cloned.1.call-update) | async-done | bytes 131088 | tf_op jit(solution)/shard_map/reduce_scatter | solution.py:495
  1357.3 66.8 %reduce-scatter.20.cloned.1.call-done = f32[128,256]{1,0:T(8,128)} async-done(((f32[1024,256]{1,0:T(8,128)}), f32[128,256]{1,0:T(8,128)}) %reduce-scatter.20.cloned.1.call-update) | async-done | bytes 131088 | tf_op jit(solution)/shard_map/reduce_scatter | solution.py:496
  (622 shorter events, 285.5 us)
Async XLA Ops:
  7.2 226.8 %all-gather.10.cloned.1.call-start = ((), (), s32[]{:S(2)}) async-start(), calls=%async_computation.11 | async-start | bytes 1769472 | tf_op jit(solution)/shard_map/all_gather | solution.py:157
  7.9 340.4 %all-reduce.10.cloned.1.call-start = ((), (), s32[]{:S(2)}) async-start(), calls=%async_computation.12 | async-start | bytes 2097152 | tf_op jit(solution)/shard_map/psum | solution.py:307
  8.0 86.0 %copy-start.110 = (f32[32]{0:T(128)}, f32[32]{0:T(128)S(1)}, u32[]{:S(2)}) copy-start(f32[32]{0:T(128)S(1)} %negate_power_fusion) | copy-start | bytes 388
  10.1 227.3 %copy-start.95 = (f32[512]{0:T(512)}, f32[512]{0:T(512)S(1)}, u32[]{:S(2)}) copy-start(f32[512]{0:T(512)S(1)} %get-tuple-element.1950) | copy-start | bytes 6148
  32.4 205.0 %copy-start.84 = (f32[8,1,128]{2,1,0:T(1,128)}, f32[8,1,128]{2,1,0:T(1,128)S(1)}, u32[]{:S(2)}) copy-start(f32[8,1,128]{2,1,0:T(1,128)S(1)} %convert_element_type.307) | copy-start | bytes 12292
  33.1 61.3 %copy-start.91 = (f32[512]{0:T(512)}, f32[512]{0:T(512)S(1)}, u32[]{:S(2)}) copy-start(f32[512]{0:T(512)S(1)} %fusion.250) | copy-start | bytes 6148
  33.1 137.6 %copy-start.102 = (f32[512]{0:T(512)}, f32[512]{0:T(512)S(1)}, u32[]{:S(2)}) copy-start(f32[512]{0:T(512)S(1)} %fusion.252) | copy-start | bytes 6148
  33.8 137.0 %copy-start.113 = (f32[6]{0:T(128)}, f32[6]{0:T(128)S(1)}, u32[]{:S(2)}) copy-start(f32[6]{0:T(128)S(1)} %exponential_negate_fusion) | copy-start | bytes 76
  60.1 75.9 %copy-start.79 = (bf16[1024,6]{0,1:T(8,128)(2,1)}, bf16[1024,6]{0,1:T(8,128)(2,1)S(1)}, u32[]{:S(2)}) copy-start(bf16[1024,6]{0,1:T(8,128)(2,1)S(1)} %all_gather.70) | copy-start | bytes 36868
  136.1 66.7 %copy-start.24 = (bf16[512,2,64]{0,2,1:T(8,128)(2,1)}, bf16[512,2,64]{0,2,1:T(8,128)(2,1)S(1)}, u32[]{:S(2)}) copy-start(bf16[512,2,64]{0,2,1:T(8,128)(2,1)S(1)} %get-tuple-element.2936) | copy-start | bytes 393220
  136.6 66.2 %copy-start.81 = (f32[512,6]{0,1:T(8,128)}, f32[512,6]{0,1:T(8,128)S(1)}, u32[]{:S(2)}) copy-start(f32[512,6]{0,1:T(8,128)S(1)} %get-tuple-element.1954) | copy-start | bytes 36868
  143.4 60.1 %copy-start.42 = (bf16[512,2,64]{0,2,1:T(8,128)(2,1)}, bf16[512,2,64]{0,2,1:T(8,128)(2,1)S(1)}, u32[]{:S(2)}) copy-start(bf16[512,2,64]{0,2,1:T(8,128)(2,1)S(1)} %convert_element_type.267) | copy-start | bytes 393220
  170.8 79.3 %copy-start.67 = (f32[512,6]{0,1:T(8,128)}, f32[512,6]{0,1:T(8,128)S(1)}, u32[]{:S(2)}) copy-start(f32[512,6]{0,1:T(8,128)S(1)} %get-tuple-element.1900) | copy-start | bytes 36868
  313.6 77.6 %all-gather.12.cloned.1.call-start = ((), (), s32[]{:S(2)}) async-start(), calls=%async_computation.13 | async-start | bytes 1179648 | tf_op jit(solution)/shard_map/all_gather | solution.py:164
  314.4 118.0 %all-gather.14.cloned.1.call-start = ((), (), s32[]{:S(2)}) async-start(), calls=%async_computation.14 | async-start | bytes 1179648 | tf_op jit(solution)/shard_map/all_gather | solution.py:165
  314.9 157.9 %all-gather.16.cloned.1.call-start = ((), (), s32[]{:S(2)}) async-start(), calls=%async_computation.15 | async-start | bytes 1179648 | tf_op jit(solution)/shard_map/all_gather | solution.py:166
  315.5 200.0 %all-reduce.12.cloned.1.call-start = ((), (), s32[]{:S(2)}) async-start(), calls=%async_computation.16 | async-start | bytes 2097152 | tf_op jit(solution)/shard_map/psum | solution.py:355
  332.7 185.7 %copy-start.73 = (f32[8,1,128]{2,1,0:T(1,128)}, f32[8,1,128]{2,1,0:T(1,128)S(1)}, u32[]{:S(2)}) copy-start(f32[8,1,128]{2,1,0:T(1,128)S(1)} %convert_element_type.308) | copy-start | bytes 12292
  350.1 168.3 %copy-start.89 = (f32[512]{0:T(512)}, f32[512]{0:T(512)S(1)}, u32[]{:S(2)}) copy-start(f32[512]{0:T(512)S(1)} %get-tuple-element.1952) | copy-start | bytes 6148
  350.1 168.3 %copy-start.98 = (f32[512]{0:T(512)}, f32[512]{0:T(512)S(1)}, u32[]{:S(2)}) copy-start(f32[512]{0:T(512)S(1)} %get-tuple-element.1951) | copy-start | bytes 6148
  480.4 180.9 %reduce-scatter.12.cloned.1.call-start = ((), (), s32[]{:S(2)}) async-start(), calls=%async_computation.17 | async-start | bytes 393216 | tf_op jit(solution)/shard_map/reduce_scatter | solution.py:432
  643.3 99.2 %all-reduce.14.cloned.1.call-start = ((), (), s32[]{:S(2)}) async-start(), calls=%async_computation.28 | async-start | bytes 6291456 | tf_op jit(solution)/shard_map/psum | solution.py:314
  668.8 153.1 %reduce-scatter.14.cloned.1.call-start = ((), (), s32[]{:S(2)}) async-start(), calls=%async_computation.18 | async-start | bytes 3538944 | tf_op jit(solution)/shard_map/reduce_scatter | solution.py:493
  672.9 205.5 %reduce-scatter.16.cloned.1.call-start = ((), (), s32[]{:S(2)}) async-start(), calls=%async_computation.19 | async-start | bytes 36864 | tf_op jit(solution)/shard_map/reduce_scatter | solution.py:494
  674.0 270.2 %reduce-scatter.26.cloned.1.call-start = ((), (), s32[]{:S(2)}) async-start(), calls=%async_computation.24 | async-start | bytes 589824 | tf_op jit(solution)/shard_map/reduce_scatter | solution.py:499
  675.2 333.8 %reduce-scatter.22.cloned.1.call-start = ((), (), s32[]{:S(2)}) async-start(), calls=%async_computation.22 | async-start | bytes 589824 | tf_op jit(solution)/shard_map/reduce_scatter | solution.py:497
  676.7 401.3 %reduce-scatter.24.cloned.1.call-start = ((), (), s32[]{:S(2)}) async-start(), calls=%async_computation.23 | async-start | bytes 1769472 | tf_op jit(solution)/shard_map/reduce_scatter | solution.py:498
  678.6 470.3 %reduce-scatter.28.cloned.1.call-start = ((), (), s32[]{:S(2)}) async-start(), calls=%async_computation.25 | async-start | bytes 2359296 | tf_op jit(solution)/shard_map/reduce_scatter | solution.py:500
  682.0 537.7 %reduce-scatter.30.cloned.1.call-start = ((), (), s32[]{:S(2)}) async-start(), calls=%async_computation.26 | async-start | bytes 2359296 | tf_op jit(solution)/shard_map/reduce_scatter | solution.py:501
  685.5 605.5 %reduce-scatter.32.cloned.1.call-start = ((), (), s32[]{:S(2)}) async-start(), calls=%async_computation.27 | async-start | bytes 2359296 | tf_op jit(solution)/shard_map/reduce_scatter | solution.py:502
  688.6 668.7 %reduce-scatter.18.cloned.1.call-start = ((), (), s32[]{:S(2)}) async-start(), calls=%async_computation.20 | async-start | bytes 1179648 | tf_op jit(solution)/shard_map/reduce_scatter | solution.py:495
  744.7 679.4 %reduce-scatter.20.cloned.1.call-start = ((), (), s32[]{:S(2)}) async-start(), calls=%async_computation.21 | async-start | bytes 1179648 | tf_op jit(solution)/shard_map/reduce_scatter | solution.py:496
  (127 other events, 925.4 us)
Sparse Core Ops, SparseCore 0:
  10.2 47.3 all-gather.9
  313.7 34.5 all-reduce.9
  350.7 40.5 all-gather.11
  393.5 38.8 all-gather.13
  434.5 38.2 all-gather.15
  480.5 34.9 all-reduce.11
  643.4 16.2 reduce-scatter.11
  668.9 73.5 all-reduce.13
  746.5 75.3 reduce-scatter.13
  825.8 52.5 reduce-scatter.15
  882.7 61.4 reduce-scatter.25
  948.0 60.8 reduce-scatter.21
  1013.4 64.6 reduce-scatter.23
  1082.0 66.8 reduce-scatter.27
  1152.8 66.7 reduce-scatter.29
  1223.6 67.2 reduce-scatter.31
  1294.8 62.4 reduce-scatter.17
  1361.5 62.5 reduce-scatter.19
where the time goes:
time: 1440 us; the launch traced here: 1430 us
  waiting for transfers between devices  856 us (59%)
  blocking collectives  259 us (18%)
  local copies, waits for them, and re-layouts  113 us (8%)
  matrix products  111 us (8%)
  other arithmetic  71.7 us (5%)
  between operations  17.3 us (1%)
    reduce_scatter x1, waiting for transfers between devices, per_device(): lax.psum_scatter(down_grad, ('fsdp', 'ctx'), scatter_dimension=1, tiled=T...  71.3 us
    reduce_scatter x1, waiting for transfers between devices, per_device(): lax.psum_scatter(gate_grad, ('fsdp', 'ctx'), scatter_dimension=0, tiled=T...  70.8 us
    reduce_scatter x1, waiting for transfers between devices, per_device(): lax.psum_scatter(up_grad, ('fsdp', 'ctx'), scatter_dimension=0, tiled=True)  70.8 us
    reduce_scatter x1, waiting for transfers between devices, per_device(): lax.psum_scatter(mixer_out_grad, ('fsdp', 'ctx'), scatter_dimension=1, ti...  69.1 us
    reduce_scatter x1, waiting for transfers between devices, per_device(): lax.psum_scatter(keyval_grad, ('fsdp', 'ctx'), scatter_dimension=0, tiled...  66.8 us
    reduce_scatter x1, waiting for transfers between devices, per_device(): lax.psum_scatter(state_grad, ('fsdp', 'ctx'), scatter_dimension=0, tiled=...  66.3 us
    reduce_scatter x1, waiting for transfers between devices, per_device(): lax.psum_scatter(attn_out_grad, ('fsdp', 'ctx'), scatter_dimension=1, til...  65.8 us
    dynamic_update_slice x32, local copies, waits for them, and re-layouts, state_space(): lax.scan(advance, state_in, (log_decay.reshape(block_count, STRETCH, head...  64.8 us
  transfers between devices with their start and end apart: 18, of which 16 were waited for; matrix products, arithmetic and copies ran while one was open for 6% of the time, Pallas kernels for 0%

commit v1 on v0

--- a/solution.py
+++ b/solution.py
@@ -138,37 +138,43 @@
     ffn_up,
     ffn_down,
 ):
-    (
-        gain_in,
-        gain_ffn,
-        full_mixer_in,
-        full_step,
-        full_state,
-        full_keyval,
-        full_query,
-        full_mixer_out,
-        full_attn_out,
-        full_gate,
-        full_up,
-        full_down,
-    ) = (
-        lax.all_gather(in_norm_gain, ("fsdp", "ctx"), axis=0, tiled=True),
-        lax.all_gather(ffn_norm_gain, ("fsdp", "ctx"), axis=0, tiled=True),
-        lax.all_gather(mixer_in, ("fsdp", "ctx"), axis=0, tiled=True),
-        lax.all_gather(step_weight, ("fsdp", "ctx"), axis=0, tiled=True),
-        lax.all_gather(state_proj, ("fsdp", "ctx"), axis=0, tiled=True),
-        lax.all_gather(keyval_weight, ("fsdp", "ctx"), axis=0, tiled=True),
-        lax.all_gather(query_weight, ("fsdp", "ctx"), axis=0, tiled=True),
-        lax.all_gather(mixer_out, ("fsdp", "ctx"), axis=1, tiled=True),
-        lax.all_gather(attn_out, ("fsdp", "ctx"), axis=1, tiled=True),
-        lax.all_gather(ffn_gate, ("fsdp", "ctx"), axis=0, tiled=True),
-        lax.all_gather(ffn_up, ("fsdp", "ctx"), axis=0, tiled=True),
-        lax.all_gather(ffn_down, ("fsdp", "ctx"), axis=1, tiled=True),
-    )
-    width_model = full_gate.shape[0]
-    row_count = tokens.shape[1]
     heads_here = step_weight.shape[1]
     inner_here = heads_here * MDIM
+    query_cols = query_weight.shape[1]
+    hidden_here = ffn_gate.shape[1]
+    state_span = state_proj.shape[1]
+    keyval_span = keyval_weight.shape[1]
+    shard_rows = tokens.shape[2] // (lax.axis_size("fsdp") * lax.axis_size("ctx"))
+    weights_in = jnp.concatenate(
+        [
+            mixer_in.reshape(shard_rows, -1),
+            state_proj,
+            keyval_weight,
+            query_weight,
+            step_weight,
+            in_norm_gain[:, None],
+            ffn_norm_gain[:, None],
+        ],
+        axis=1,
+    )
+    weights_out = jnp.concatenate([mixer_out.T, attn_out.T, ffn_down.T, ffn_gate, ffn_up], axis=1)
+    full_in = lax.all_gather(weights_in, ("fsdp", "ctx"), axis=0, tiled=True)
+    full_out = lax.all_gather(weights_out, ("fsdp", "ctx"), axis=0, tiled=True)
+    mix_end = 2 * inner_here
+    state_end = mix_end + state_span
+    keyval_end = state_end + keyval_span
+    query_end = keyval_end + query_cols
+    step_end = query_end + heads_here
+    gain_in = full_in[:, step_end]
+    gain_ffn = full_in[:, step_end + 1]
+    attn_end = inner_here + query_cols
+    down_end = attn_end + hidden_here
+    gate_end = down_end + hidden_here
+    full_mixers_t = full_out[:, :attn_end]
+    full_down_t = full_out[:, attn_end:down_end]
+    full_gate_up = full_out[:, down_end:]
+    width_model = full_out.shape[0]
+    row_count = tokens.shape[1]
     query_here = query_weight.shape[1] // HDIM
     kv_span = KVHEADS * HDIM
     ctx_index = lax.axis_index("ctx")
@@ -179,23 +185,18 @@
     inputs_f = tokens[0].astype(jnp.float32)
     inv_one = lax.rsqrt(jnp.mean(inputs_f * inputs_f, axis=-1, keepdims=True) + EPS)
     normed = (inputs_f * inv_one * gain_in.astype(jnp.float32)).astype(jnp.bfloat16)
-    mixer_flat = full_mixer_in.reshape(width_model, -1)
-    projected = jnp.dot(normed, mixer_flat, preferred_element_type=jnp.float32).reshape(
-        row_count, 2, heads_here, MDIM
-    )
+    all_cols = jnp.dot(normed, full_in[:, :step_end], preferred_element_type=jnp.float32)
+    projected = all_cols[:, :mix_end].reshape(row_count, 2, heads_here, MDIM)
     gate_pre = projected[:, 0]
     inputs = projected[:, 1]
-    step_raw = jnp.dot(normed, full_step, preferred_element_type=jnp.float32)
-    state_cols = jnp.dot(normed, full_state, preferred_element_type=jnp.float32)
-    b_proj = state_cols[:, :STATE]
-    c_proj = state_cols[:, STATE:]
-    keyval_cols = jnp.dot(normed, full_keyval, preferred_element_type=jnp.float32)
+    step_raw = all_cols[:, query_end:]
+    b_proj = all_cols[:, mix_end : mix_end + STATE]
+    c_proj = all_cols[:, mix_end + STATE : state_end]
+    keyval_cols = all_cols[:, state_end:keyval_end]
     kv_head = tp_index * query_here // (QHEADS // KVHEADS)
     key_raw = lax.dynamic_slice_in_dim(keyval_cols, kv_head * HDIM, HDIM, 1)
     value_raw = lax.dynamic_slice_in_dim(keyval_cols, kv_span + kv_head * HDIM, HDIM, 1)
-    queries = jnp.dot(normed, full_query, preferred_element_type=jnp.float32).reshape(
-        row_count, query_here, HDIM
-    )
+    queries = all_cols[:, keyval_end:query_end].reshape(row_count, query_here, HDIM)
     query_b = rotate(queries, places).astype(jnp.bfloat16)
     key_b = rotate(key_raw[:, None, :], places)[:, 0].astype(jnp.bfloat16)
     own_keyval = jnp.concatenate([key_b, value_raw.astype(jnp.bfloat16)], axis=1)
@@ -241,7 +242,7 @@
             state_part,
         )
 
-    (gated, state_end), mixer_back = jax.vjp(
+    (gated, state_last), mixer_back = jax.vjp(
         mixer_fn,
         inputs,
         gate_pre,
@@ -301,64 +302,33 @@
         0, block_count, weighted_sum, jnp.zeros((row_count, query_here, HDIM), jnp.float32)
     ).astype(jnp.bfloat16)
     attn_flat_b = attended_b.reshape(row_count, query_here * HDIM)
-    partial_term = jnp.dot(gated_b, full_mixer_out, preferred_element_type=jnp.float32) + jnp.dot(
-        attn_flat_b, full_attn_out, preferred_element_type=jnp.float32
-    )
+    mixers_b = jnp.concatenate([gated_b, attn_flat_b], axis=1)
+    partial_term = jnp.dot(mixers_b, full_mixers_t.T, preferred_element_type=jnp.float32)
     mixed = lax.psum(partial_term.astype(jnp.bfloat16), "tp").astype(jnp.float32)
     resid = inputs_f + mixed
     inv_two = lax.rsqrt(jnp.mean(resid * resid, axis=-1, keepdims=True) + EPS)
     normed_two = (resid * inv_two * gain_ffn.astype(jnp.float32)).astype(jnp.bfloat16)
-    gate_val = jnp.dot(normed_two, full_gate, preferred_element_type=jnp.float32)
-    up_val = jnp.dot(normed_two, full_up, preferred_element_type=jnp.float32)
+    gate_up = jnp.dot(normed_two, full_gate_up, preferred_element_type=jnp.float32)
+    gate_val = gate_up[:, :hidden_here]
+    up_val = gate_up[:, hidden_here:]
     act_b = (jax.nn.silu(gate_val) * up_val).astype(jnp.bfloat16)
-    ffn_total = lax.psum(
-        jnp.dot(act_b, full_down, preferred_element_type=jnp.float32).astype(jnp.bfloat16), "tp"
-    ).astype(jnp.float32)
-    block_out = (resid + ffn_total).astype(jnp.bfloat16)
-    (
-        gain_in,
-        gain_ffn,
-        full_mixer_in,
-        full_step,
-        full_state,
-        full_keyval,
-        full_query,
-        full_mixer_out,
-        full_attn_out,
-        full_gate,
-        full_up,
-        full_down,
-    ) = (
-        lax.all_gather(in_norm_gain, ("fsdp", "ctx"), axis=0, tiled=True),
-        lax.all_gather(ffn_norm_gain, ("fsdp", "ctx"), axis=0, tiled=True),
-        lax.all_gather(mixer_in, ("fsdp", "ctx"), axis=0, tiled=True),
-        lax.all_gather(step_weight, ("fsdp", "ctx"), axis=0, tiled=True),
-        lax.all_gather(state_proj, ("fsdp", "ctx"), axis=0, tiled=True),
-        lax.all_gather(keyval_weight, ("fsdp", "ctx"), axis=0, tiled=True),
-        lax.all_gather(query_weight, ("fsdp", "ctx"), axis=0, tiled=True),
-        lax.all_gather(mixer_out, ("fsdp", "ctx"), axis=1, tiled=True),
-        lax.all_gather(attn_out, ("fsdp", "ctx"), axis=1, tiled=True),
-        lax.all_gather(ffn_gate, ("fsdp", "ctx"), axis=0, tiled=True),
-        lax.all_gather(ffn_up, ("fsdp", "ctx"), axis=0, tiled=True),
-        lax.all_gather(ffn_down, ("fsdp", "ctx"), axis=1, tiled=True),
-    )
+    ffn_term = jnp.dot(act_b, full_down_t.T, preferred_element_type=jnp.float32)
     cot_rows = cotangent[0]
-    act_grad = jnp.dot(cot_rows, full_down.T, preferred_element_type=jnp.float32)
+    act_grad = jnp.dot(cot_rows, full_down_t, preferred_element_type=jnp.float32)
     sigmoid_gate = jax.nn.sigmoid(gate_val)
     dgate_b = (act_grad * up_val * sigmoid_gate * (1.0 + gate_val * (1.0 - sigmoid_gate))).astype(
         jnp.bfloat16
     )
     dup_b = (act_grad * gate_val * sigmoid_gate).astype(jnp.bfloat16)
-    down_grad = jnp.dot(act_b.T, cot_rows, preferred_element_type=jnp.float32)
-    gate_grad = jnp.dot(normed_two.T, dgate_b, preferred_element_type=jnp.float32)
-    up_grad = jnp.dot(normed_two.T, dup_b, preferred_element_type=jnp.float32)
-    dnormed_two = lax.psum(
-        (
-            jnp.dot(dgate_b, full_gate.T, preferred_element_type=jnp.float32)
-            + jnp.dot(dup_b, full_up.T, preferred_element_type=jnp.float32)
-        ).astype(jnp.bfloat16),
-        "tp",
+    dgate_up_b = jnp.concatenate([dgate_b, dup_b], axis=1)
+    down_grad_t = jnp.dot(cot_rows.T, act_b, preferred_element_type=jnp.float32)
+    gate_up_grad = jnp.dot(normed_two.T, dgate_up_b, preferred_element_type=jnp.float32)
+    dnormed_two_term = jnp.dot(dgate_up_b, full_gate_up.T, preferred_element_type=jnp.float32)
+    ffn_sums = lax.psum(
+        jnp.concatenate([dnormed_two_term, ffn_term], axis=1).astype(jnp.bfloat16), "tp"
     ).astype(jnp.float32)
+    dnormed_two = ffn_sums[:, :width_model]
+    block_out = (resid + ffn_sums[:, width_model:]).astype(jnp.bfloat16)
     scaled_two = gain_ffn.astype(jnp.float32) * dnormed_two
     ffn_norm_grad = jnp.sum(dnormed_two * resid * inv_two, axis=0)
     dresid = (
@@ -367,15 +337,19 @@
         - resid * inv_two**3 * jnp.mean(scaled_two * resid, axis=-1, keepdims=True)
     )
     dmixed_b = dresid.astype(jnp.bfloat16)
-    mixer_out_grad = jnp.dot(gated_b.T, dmixed_b, preferred_element_type=jnp.float32)
-    attn_out_grad = jnp.dot(attn_flat_b.T, dmixed_b, preferred_element_type=jnp.float32)
-    dgated = jnp.dot(dmixed_b, full_mixer_out.T, preferred_element_type=jnp.float32).reshape(
-        row_count, heads_here, MDIM
-    )
+    mixers_grad_t = jnp.dot(dmixed_b.T, mixers_b, preferred_element_type=jnp.float32)
+    out_rows = lax.psum_scatter(
+        jnp.concatenate(
+            [mixers_grad_t, down_grad_t, gate_up_grad, ffn_norm_grad[:, None]], axis=1
+        ).astype(jnp.bfloat16),
+        ("fsdp", "ctx"),
+        scatter_dimension=0,
+        tiled=True,
+    ).astype(jnp.float32)
+    dmixers = jnp.dot(dmixed_b, full_mixers_t, preferred_element_type=jnp.float32)
+    dgated = dmixers[:, :inner_here].reshape(row_count, heads_here, MDIM)
     dattended_b = (
-        jnp.dot(dmixed_b, full_attn_out.T, preferred_element_type=jnp.float32)
-        .reshape(row_count, query_here, HDIM)
-        .astype(jnp.bfloat16)
+        dmixers[:, inner_here:].reshape(row_count, query_here, HDIM).astype(jnp.bfloat16)
     )
     dstate_direct = jnp.einsum(
         "sn,sh,shp->hnp",
@@ -429,9 +403,13 @@
             jnp.zeros((all_keyval.shape[0], 2 * HDIM), jnp.float32),
         ),
     )
-    own_dkeyval = lax.psum_scatter(
-        dkeyval.astype(jnp.bfloat16), "ctx", scatter_dimension=0, tiled=True
-    ).astype(jnp.float32)
+    all_dkeyval = lax.all_gather(dkeyval.astype(jnp.bfloat16), "ctx", axis=0)
+    own_dkeyval = jnp.sum(
+        lax.dynamic_slice_in_dim(all_dkeyval, ctx_index * row_count, row_count, 1).astype(
+            jnp.float32
+        ),
+        axis=0,
+    )
     dkey_rot = rotate_back(own_dkeyval[:, None, :HDIM], places)[:, 0]
     dkeyval_full = jnp.zeros((row_count, 2 * kv_span), jnp.float32)
     dkeyval_full = lax.dynamic_update_slice_in_dim(dkeyval_full, dkey_rot, kv_head * HDIM, 1)
@@ -449,20 +427,20 @@
         .astype(jnp.bfloat16)
     )
     dstep_b = dstep_raw.astype(jnp.bfloat16)
-    mixer_in_grad = jnp.dot(normed.T, dmix_in_b, preferred_element_type=jnp.float32).reshape(
-        width_model, 2, inner_here
-    )
-    step_grad = jnp.dot(normed.T, dstep_b, preferred_element_type=jnp.float32)
-    state_grad = jnp.dot(normed.T, dstate_b, preferred_element_type=jnp.float32)
-    keyval_grad = jnp.dot(normed.T, dkeyval_b, preferred_element_type=jnp.float32)
-    query_grad = jnp.dot(normed.T, dquery_b, preferred_element_type=jnp.float32)
-    back_flat = full_mixer_in.reshape(width_model, -1)
-    group_term = jnp.dot(dmix_in_b, back_flat.T, preferred_element_type=jnp.float32)
-    group_term = group_term + jnp.dot(dstep_b, full_step.T, preferred_element_type=jnp.float32)
-    group_term = group_term + jnp.dot(dstate_b, full_state.T, preferred_element_type=jnp.float32)
-    group_term = group_term + jnp.dot(dkeyval_b, full_keyval.T, preferred_element_type=jnp.float32)
-    group_term = group_term + jnp.dot(dquery_b, full_query.T, preferred_element_type=jnp.float32)
-    dnormed = lax.psum(group_term.astype(jnp.bfloat16), "tp").astype(jnp.float32)
+    shared_b = jnp.concatenate([dstate_b, dkeyval_b], axis=1)
+    dcols_b = jnp.concatenate([dmix_in_b, shared_b, dquery_b, dstep_b], axis=1)
+    group_term = jnp.dot(dcols_b, full_in[:, :step_end].T, preferred_element_type=jnp.float32)
+    group_sums = lax.psum(
+        jnp.concatenate([group_term.astype(jnp.bfloat16), shared_b], axis=1), "tp"
+    )
+    dnormed = group_sums[:, :width_model].astype(jnp.float32)
+    shared_sum = group_sums[:, width_model:]
+    own_grad = jnp.dot(
+        normed.T,
+        jnp.concatenate([dmix_in_b, dquery_b, dstep_b], axis=1),
+        preferred_element_type=jnp.float32,
+    )
+    shared_grad = jnp.dot(normed.T, shared_sum, preferred_element_type=jnp.float32)
     scaled_one = gain_in.astype(jnp.float32) * dnormed
     in_norm_grad = jnp.sum(dnormed * inputs_f * inv_one, axis=0)
     input_grad = (
@@ -470,38 +448,37 @@
         + inv_one * scaled_one
         - inputs_f * inv_one**3 * jnp.mean(scaled_one * inputs_f, axis=-1, keepdims=True)
     )
-    state_grad, keyval_grad = (
-        lax.psum(state_grad.astype(jnp.bfloat16), "tp").astype(jnp.float32),
-        lax.psum(keyval_grad.astype(jnp.bfloat16), "tp").astype(jnp.float32),
-    )
-    (
-        in_norm_rows,
-        ffn_norm_rows,
-        mixer_in_rows,
-        step_rows,
-        state_rows,
-        keyval_rows,
-        query_rows,
-        mixer_out_rows,
-        attn_out_rows,
-        gate_rows,
-        up_rows,
-        down_rows,
-    ) = (
-        lax.psum_scatter(in_norm_grad, ("fsdp", "ctx"), scatter_dimension=0, tiled=True),
-        lax.psum_scatter(ffn_norm_grad, ("fsdp", "ctx"), scatter_dimension=0, tiled=True),
-        lax.psum_scatter(mixer_in_grad, ("fsdp", "ctx"), scatter_dimension=0, tiled=True),
-        lax.psum_scatter(step_grad, ("fsdp", "ctx"), scatter_dimension=0, tiled=True),
-        lax.psum_scatter(state_grad, ("fsdp", "ctx"), scatter_dimension=0, tiled=True),
-        lax.psum_scatter(keyval_grad, ("fsdp", "ctx"), scatter_dimension=0, tiled=True),
-        lax.psum_scatter(query_grad, ("fsdp", "ctx"), scatter_dimension=0, tiled=True),
-        lax.psum_scatter(mixer_out_grad, ("fsdp", "ctx"), scatter_dimension=1, tiled=True),
-        lax.psum_scatter(attn_out_grad, ("fsdp", "ctx"), scatter_dimension=1, tiled=True),
-        lax.psum_scatter(gate_grad, ("fsdp", "ctx"), scatter_dimension=0, tiled=True),
-        lax.psum_scatter(up_grad, ("fsdp", "ctx"), scatter_dimension=0, tiled=True),
-        lax.psum_scatter(down_grad, ("fsdp", "ctx"), scatter_dimension=1, tiled=True),
-    )
-    bias_grad, decay_grad, skip_grad = lax.psum((dbias, ddecay, dskip), ("fsdp", "ctx"))
+    head_columns = jnp.tile(
+        jnp.pad(jnp.stack([dbias, ddecay, dskip], axis=1), ((0, shard_rows - heads_here), (0, 0))),
+        (width_model // shard_rows, 1),
+    )
+    in_rows = lax.psum_scatter(
+        jnp.concatenate(
+            [own_grad, shared_grad, in_norm_grad[:, None], head_columns], axis=1
+        ).astype(jnp.bfloat16),
+        ("fsdp", "ctx"),
+        scatter_dimension=0,
+        tiled=True,
+    ).astype(jnp.float32)
+    query_stop = mix_end + query_cols
+    step_stop = query_stop + heads_here
+    state_stop = step_stop + state_span
+    keyval_stop = state_stop + keyval_span
+    mixer_in_rows = in_rows[:, :mix_end].reshape(shard_rows, 2, inner_here)
+    query_rows = in_rows[:, mix_end:query_stop]
+    step_rows = in_rows[:, query_stop:step_stop]
+    state_rows = in_rows[:, step_stop:state_stop]
+    keyval_rows = in_rows[:, state_stop:keyval_stop]
+    in_norm_rows = in_rows[:, keyval_stop]
+    bias_grad = in_rows[:heads_here, keyval_stop + 1]
+    decay_grad = in_rows[:heads_here, keyval_stop + 2]
+    skip_grad = in_rows[:heads_here, keyval_stop + 3]
+    mixer_out_rows = out_rows[:, :inner_here].T
+    attn_out_rows = out_rows[:, inner_here:attn_end].T
+    down_rows = out_rows[:, attn_end:down_end].T
+    gate_rows = out_rows[:, down_end:gate_end]
+    up_rows = out_rows[:, gate_end : gate_end + hidden_here]
+    ffn_norm_rows = out_rows[:, gate_end + hidden_here]
     return (
         block_out[None],
         input_grad[None],

time: 1440 us -> 764 us (0.53)
  waiting for transfers between devices: 856 us -> 327 us
  blocking collectives: 259 us -> 39.2 us
  local copies, waits for them, and re-layouts: 113 us -> 198 us
  matrix products: 111 us -> 75 us
  other arithmetic: 71.7 us -> 93.1 us
    reduce_scatter x11 -> x0, waiting for transfers between devices: 643 us -> none  [the longest x1 71.3 us: per_device(): lax.psum_scatter(down_grad, ('fsdp', 'ctx'), scatter_dimension=1, tiled=T...]
    all_gather x8 -> x1, blocking collectives: 215 us -> 11.7 us  [per_device(): all_dkeyval = lax.all_gather(dkeyval.astype(jnp.bfloat16), 'ctx', axis=0)]
    unnamed x18 -> x9, waiting for transfers between devices: 2.65 us -> 145 us
    all_gather x4 -> x2, waiting for transfers between devices: 115 us -> 58.1 us  [the longest x1 58.1 us: per_device(): full_in = lax.all_gather(weights_in, ('fsdp', 'ctx'), axis=0, tiled=True)]
    dot_general x30 -> x13, matrix products: 60.8 us -> 27.6 us  [the longest x1 3.63 us: per_device(): jnp.dot(normed, full_in[:, :step_end], preferred_element_type=jnp.float32)]
    unnamed x1 -> x0, blocking collectives: 23.5 us -> none
    psum x1, waiting for transfers between devices: 15.6 us -> 36.9 us  [per_device(): lax.psum(partial_term.astype(jnp.bfloat16), 'tp').astype(jnp.float32)]
    unnamed x208 -> x213, local copies, waits for them, and re-layouts: 14.2 us -> 34.3 us
  transfers between devices with their start and end apart: 18 -> 7, of which waited for: 16 -> 6; matrix products, arithmetic and copies ran while one was open for 6% -> 16% of each run, Pallas kernels for 0% -> 0%
where the time goes in v1:
time: 764 us; the launch traced here: 752 us
  waiting for transfers between devices  327 us (43%)
  local copies, waits for them, and re-layouts  198 us (26%)
  other arithmetic  93.1 us (12%)
  matrix products  75 us (10%)
  blocking collectives  39.2 us (5%)
  between operations  16.8 us (2%)
    unnamed x9, waiting for transfers between devices  145 us
    dynamic_update_slice x32, local copies, waits for them, and re-layouts, state_space(): lax.scan(advance, state_in, (log_decay.reshape(block_count, STRETCH, head...  66.6 us
    all_gather x1, waiting for transfers between devices, per_device(): full_in = lax.all_gather(weights_in, ('fsdp', 'ctx'), axis=0, tiled=True)  58.1 us
    psum x1, waiting for transfers between devices, per_device(): lax.psum(jnp.concatenate([dnormed_two_term, ffn_term], axis=1).astype(jnp...  46.5 us
    psum x1, waiting for transfers between devices, per_device(): lax.psum(jnp.concatenate([group_term.astype(jnp.bfloat16), shared_b], axi...  40 us
    psum x1, waiting for transfers between devices, per_device(): lax.psum(partial_term.astype(jnp.bfloat16), 'tp').astype(jnp.float32)  36.9 us
    unnamed x213, local copies, waits for them, and re-layouts  34.3 us
    another operation x26, other arithmetic  32.4 us
  transfers between devices with their start and end apart: 7, of which 6 were waited for; matrix products, arithmetic and copies ran while one was open for 16% of the time, Pallas kernels for 0%

profile of v1, /device:TPU:0, one launch (start us, length us, event | category | flops | bytes accessed | tf_op | source)
XLA Modules:
  0.0 751.5 jit_solution(9412893512149082827)
XLA Ops:
  11.3 3.9 concatenate.61
  20.2 58.1 %all-gather.7.cloned.1.call-done = bf16[1024,1416]{0,1:T(8,128)(2,1)} async-done(((bf16[128,1416]{0,1:T(8,128)(2,1)}), bf16[1024,1416]{0,1:T(8,128)(2,1)}) %all-gather.7.cloned.1.call-update) | async-done | bytes 2899984 | tf_op jit(solution)/shard_map/all_gather | solution.py:161
  79.7 3.6 fusion.155
  93.0 5.8 all_gather.37
  104.6 8.8 %all-gather.3 = bf16[2,1,6]{2,1,0:T(2,128)(2,1)S(1)} all-gather(bf16[1,1,6]{2,1,0:T(2,128)(2,1)S(1)} %bitcast.784), channel_id=1, replica_groups=mesh['fsdp'=4,'ctx'=2,'tp'=4] {'ctx'}, dimensions={0}, use_global_device_ids=true | all-gather | bytes 36 | tf_op jit(solution)/shard_map/all_gather | solution.py:25
  116.2 7.6 %all-gather = bf16[12,128,64]{1,2,0:T(8,128)(2,1)S(1)} all-gather(bf16[6,128,64]{1,2,0:T(8,128)(2,1)S(1)} %fusion.180), channel_id=2, replica_groups=mesh['fsdp'=4,'ctx'=2,'tp'=4] {'ctx'}, dimensions={0}, use_global_device_ids=true | all-gather | bytes 294912 | tf_op jit(solution)/shard_map/all_gather | solution.py:25
  132.9 55.0 %while.134 = (s32[]{:T(128)}, f32[6,128,64]{1,2,0:T(8,128)S(1)}, f32[2,256,6,64]{1,0,3,2:T(2,128)}, f32[2,256,256,6]{2,1,3,0:T(8,128)}, f32[2,128,256]{1,2,0:T(8...) while((s32[]{:T(128)}, f32[6,128,64]{1,2,0:T(8,128)S(1)}, ...), condition=%wide.region_8.9_spmd.clone.clone, body=%wide.region_5.8_spmd.clone.clone.sunk | while | flops 708675072 | bytes 14110885 | solution.py:102
  143.3 9.0 %dynamic_update_slice.203 = f32[2,256,6,64]{1,0,3,2:T(2,128)} dynamic-update-slice(f32[2,256,6,64]{1,0,3,2:T(2,128)} %get-tuple-element.2683, f32[1,256,6,64]{1,0,3,2:T(1,128)S(1)} %copy.488, s32[]{:T(128)S(6)} %copy.565, s32[]{:T(128)} %constant.279.clone.1..sunk.5, s32[]{:T(128)} %constant.279.clone.1..sunk.5, s32[]{:T(128)} %constant.279.clone.1..sunk.5) | dynamic-update-slice | bytes 786436 | tf_op jit(solution)/shard_map/jvp()/while/body/jit(dynamic_update_index_in_dim)/dynamic_update_slice | solution.py:102
  152.2 3.2 bitcast_dynamic-update-slice_fusion.14
  170.8 9.0 %dynamic_update_slice.203 = f32[2,256,6,64]{1,0,3,2:T(2,128)} dynamic-update-slice(f32[2,256,6,64]{1,0,3,2:T(2,128)} %get-tuple-element.2683, f32[1,256,6,64]{1,0,3,2:T(1,128)S(1)} %copy.488, s32[]{:T(128)S(6)} %copy.565, s32[]{:T(128)} %constant.279.clone.1..sunk.5, s32[]{:T(128)} %constant.279.clone.1..sunk.5, s32[]{:T(128)} %constant.279.clone.1..sunk.5) | dynamic-update-slice | bytes 786436 | tf_op jit(solution)/shard_map/jvp()/while/body/jit(dynamic_update_index_in_dim)/dynamic_update_slice | solution.py:102
  179.8 3.2 bitcast_dynamic-update-slice_fusion.14
  193.5 36.9 %all-reduce.7.cloned.1.call-done = bf16[512,1024]{1,0:T(8,128)(2,1)} async-done(((bf16[512,1024]{1,0:T(8,128)(2,1)}), bf16[512,1024]{1,0:T(8,128)(2,1)}) %all-reduce.7.cloned.1.call-update) | async-done | bytes 1048592 | tf_op jit(solution)/shard_map/psum | solution.py:307
  246.0 46.5 %all-reduce.9.cloned.1.call-done = bf16[512,2048]{1,0:T(8,128)(2,1)} async-done(((bf16[512,2048]{1,0:T(8,128)(2,1)}), bf16[512,2048]{1,0:T(8,128)(2,1)}) %all-reduce.9.cloned.1.call-update) | async-done | bytes 2097168 | tf_op jit(solution)/shard_map/psum | solution.py:327
  301.6 3.4 while.133
  305.0 11.7 %all-gather.2 = bf16[2048,128]{0,1:T(8,128)(2,1)S(1)} all-gather(bf16[1024,128]{0,1:T(8,128)(2,1)S(1)} %get-tuple-element.1047), channel_id=4, replica_groups=mesh['fsdp'=4,'ctx'=2,'tp'=4] {'ctx'}, dimensions={0}, use_global_device_ids=true | all-gather | bytes 786432 | tf_op jit(solution)/shard_map/all_gather | solution.py:406
  325.6 5.3 all-gather.1
  331.7 3.1 fusion.195
  339.0 132.9 %while.135 = (s32[]{:T(128)}, f32[6]{0:T(128)}, f32[6,128,64]{1,2,0:T(8,128)S(1)}, f32[2,256,6]{1,2,0:T(8,128)}, f32[2,256,6,64]{1,0,3,2:T(2,128)}, /*index=5*/b...) while((s32[]{:T(128)}, f32[6]{0:T(128)}, ...), condition=%wide.region_30.31_spmd.clone, body=%wide.region_21.30_spmd.clone.sunk | while | flops 1413523968 | bytes 30134168 | solution.py:102
  361.9 8.8 %reduce-window.60 = f32[6,2,128]{2,1,0:T(2,128)} reduce-window(f32[6,2,128]{2,1,0:T(2,128)} %reshape.724, f32[]{:T(128)} %constant.280.clone.1..sunk.1), window={size=1x1x128 pad=0_0x0_0x0_127}, to_apply=%region_28.28 | reduce-window | flops 195072 | bytes 12292 | tf_op jit(solution)/shard_map/reduce-window.20
  380.1 9.0 %dynamic_update_slice.208 = f32[2,256,6,64]{1,0,3,2:T(2,128)} dynamic-update-slice(f32[2,256,6,64]{1,0,3,2:T(2,128)} %get-tuple-element.2837, f32[1,256,6,64]{1,0,3,2:T(1,128)S(1)} %copy.504, s32[]{:T(128)S(6)} %sub.302, s32[]{:T(128)} %constant.279.clone.1..sunk.6, s32[]{:T(128)} %constant.279.clone.1..sunk.6, s32[]{:T(128)} %constant.279.clone.1..sunk.6) | dynamic-update-slice | bytes 786436 | tf_op jit(solution)/shard_map/transpose(jvp())/while/body/jit(dynamic_update_index_in_dim)/dynamic_update_slice | solution.py:102
  396.1 9.0 %dynamic_update_slice.209 = f32[2,256,6,64]{1,0,3,2:T(2,128)} dynamic-update-slice(f32[2,256,6,64]{1,0,3,2:T(2,128)} %get-tuple-element.2840, f32[1,256,6,64]{1,0,3,2:T(1,128)S(1)} %copy.505, s32[]{:T(128)S(6)} %sub.302, s32[]{:T(128)} %constant.279.clone.1..sunk.6, s32[]{:T(128)} %constant.279.clone.1..sunk.6, s32[]{:T(128)} %constant.279.clone.1..sunk.6) | dynamic-update-slice | bytes 786436 | tf_op jit(solution)/shard_map/transpose(jvp())/while/body/jit(dynamic_update_index_in_dim)/dynamic_update_slice | solution.py:102
  428.5 8.8 %reduce-window.60 = f32[6,2,128]{2,1,0:T(2,128)} reduce-window(f32[6,2,128]{2,1,0:T(2,128)} %reshape.724, f32[]{:T(128)} %constant.280.clone.1..sunk.1), window={size=1x1x128 pad=0_0x0_0x0_127}, to_apply=%region_28.28 | reduce-window | flops 195072 | bytes 12292 | tf_op jit(solution)/shard_map/reduce-window.20
  446.7 9.0 %dynamic_update_slice.208 = f32[2,256,6,64]{1,0,3,2:T(2,128)} dynamic-update-slice(f32[2,256,6,64]{1,0,3,2:T(2,128)} %get-tuple-element.2837, f32[1,256,6,64]{1,0,3,2:T(1,128)S(1)} %copy.504, s32[]{:T(128)S(6)} %sub.302, s32[]{:T(128)} %constant.279.clone.1..sunk.6, s32[]{:T(128)} %constant.279.clone.1..sunk.6, s32[]{:T(128)} %constant.279.clone.1..sunk.6) | dynamic-update-slice | bytes 786436 | tf_op jit(solution)/shard_map/transpose(jvp())/while/body/jit(dynamic_update_index_in_dim)/dynamic_update_slice | solution.py:102
  462.7 9.0 %dynamic_update_slice.209 = f32[2,256,6,64]{1,0,3,2:T(2,128)} dynamic-update-slice(f32[2,256,6,64]{1,0,3,2:T(2,128)} %get-tuple-element.2840, f32[1,256,6,64]{1,0,3,2:T(1,128)S(1)} %copy.505, s32[]{:T(128)S(6)} %sub.302, s32[]{:T(128)} %constant.279.clone.1..sunk.6, s32[]{:T(128)} %constant.279.clone.1..sunk.6, s32[]{:T(128)} %constant.279.clone.1..sunk.6) | dynamic-update-slice | bytes 786436 | tf_op jit(solution)/shard_map/transpose(jvp())/while/body/jit(dynamic_update_index_in_dim)/dynamic_update_slice | solution.py:102
  494.7 3.6 fusion.176
  503.6 40.0 %all-reduce.11.cloned.1.call-done = bf16[512,1536]{1,0:T(8,128)(2,1)} async-done(((bf16[512,1536]{1,0:T(8,128)(2,1)}), bf16[512,1536]{1,0:T(8,128)(2,1)}) %all-reduce.11.cloned.1.call-update) | async-done | bytes 1572880 | tf_op jit(solution)/shard_map/psum | solution.py:433
  548.7 16.1 %concatenate.74 = bf16[1024,1418]{0,1:T(8,128)(2,1)} concatenate(bf16[1024,902]{0,1:T(8,128)(2,1)S(1)} %copy-done.27, bf16[1024,512]{0,1:T(8,128)(2,1)} %convolution_convert_fusion.4, bf16[1024,1]{0,1:T(2,128)(2,1)S(1)} %broadcast_in_dim.296, bf16[1024,3]{0,1:T(4,128)(2,1)S(1)} %bitcast.781), dimensions={1} | concatenate | bytes 5808128 | tf_op jit(solution)/shard_map/concatenate | solution.py:456
  564.8 4.6 copy.380
  577.1 6.4 copy.382
  584.1 3.1 fusion.160
  587.2 56.9 %reduce-scatter.7.cloned.1.call-done = bf16[128,1418]{1,0:T(8,128)(2,1)} async-done(((bf16[1024,1418]{1,0:T(8,128)(2,1)}), bf16[128,1418]{1,0:T(8,128)(2,1)}) %reduce-scatter.7.cloned.1.call-update) | async-done | bytes 363024
  650.2 88.3 %reduce-scatter.9.cloned.1.call-done = bf16[128,2049]{1,0:T(8,128)(2,1)} async-done(((bf16[1024,2049]{1,0:T(8,128)(2,1)}), bf16[128,2049]{1,0:T(8,128)(2,1)}) %reduce-scatter.9.cloned.1.call-update) | async-done | bytes 524560
  (551 shorter events, 251.0 us)
Async XLA Ops:
  7.2 9.1 %copy-start.58 = (bf16[128,512]{1,0:T(8,128)(2,1)S(1)}, bf16[128,512]{1,0:T(8,128)(2,1)}, u32[]{:S(2)}) copy-start(bf16[128,512]{1,0:T(8,128)(2,1)} %param.48) | copy-start | bytes 393220
  7.2 9.3 %copy-start.62 = (bf16[384,128]{1,0:T(8,128)(2,1)S(1)}, bf16[384,128]{1,0:T(8,128)(2,1)}, u32[]{:S(2)}) copy-start(bf16[384,128]{1,0:T(8,128)(2,1)} %param.45) | copy-start | bytes 294916
  7.2 9.3 %copy-start.69 = (bf16[128,128]{1,0:T(8,128)(2,1)S(1)}, bf16[128,128]{1,0:T(8,128)(2,1)}, u32[]{:S(2)}) copy-start(bf16[128,128]{1,0:T(8,128)(2,1)} %param.46) | copy-start | bytes 98308
  7.2 9.3 %copy-start.59 = (bf16[512,128]{1,0:T(8,128)(2,1)S(1)}, bf16[512,128]{1,0:T(8,128)(2,1)}, u32[]{:S(2)}) copy-start(bf16[512,128]{1,0:T(8,128)(2,1)} %param.49) | copy-start | bytes 393220
  7.2 10.4 %copy-start = (bf16[1,512,1024]{2,1,0:T(8,128)(2,1)S(1)}, bf16[1,512,1024]{2,1,0:T(8,128)(2,1)}, u32[]{:S(2)}) copy-start(bf16[1,512,1024]{2,1,0:T(8,128)(2,1)} %param.32) | copy-start | bytes 3145732
  7.2 71.1 %all-gather.7.cloned.1.call-start = ((), (), s32[]{:S(2)}) async-start(), calls=%async_computation.2 | async-start | bytes 3262464 | tf_op jit(solution)/shard_map/all_gather | solution.py:161
  15.3 175.1 %all-gather.9.cloned.1.call-start = ((), (), s32[]{:S(2)}) async-start(), calls=%async_computation.3 | async-start | bytes 4718592 | tf_op jit(solution)/shard_map/all_gather | solution.py:162
  17.4 213.0 %all-reduce.7.cloned.1.call-start = ((), (), s32[]{:S(2)}) async-start(), calls=%async_computation.4 | async-start | bytes 2097152 | tf_op jit(solution)/shard_map/psum | solution.py:307
  17.5 65.9 %copy-start.79 = (f32[32]{0:T(128)}, f32[32]{0:T(128)S(1)}, u32[]{:S(2)}) copy-start(f32[32]{0:T(128)S(1)} %negate_power_fusion) | copy-start | bytes 388
  18.5 64.9 %copy-start.70 = (f32[512]{0:T(512)}, f32[512]{0:T(512)S(1)}, u32[]{:S(2)}) copy-start(f32[512]{0:T(512)S(1)} %get-tuple-element.1953) | copy-start | bytes 6148
  18.5 64.9 %copy-start.68 = (f32[512]{0:T(512)}, f32[512]{0:T(512)S(1)}, u32[]{:S(2)}) copy-start(f32[512]{0:T(512)S(1)} %fusion.243) | copy-start | bytes 6148
  18.5 65.9 %copy-start.84 = (f32[6]{0:T(128)}, f32[6]{0:T(128)S(1)}, u32[]{:S(2)}) copy-start(f32[6]{0:T(128)S(1)} %exponential_negate_fusion) | copy-start | bytes 76
  19.2 65.3 %copy-start.74 = (f32[512]{0:T(512)}, f32[512]{0:T(512)S(1)}, u32[]{:S(2)}) copy-start(f32[512]{0:T(512)S(1)} %fusion.245) | copy-start | bytes 6148
  85.8 38.5 %copy-start.54 = (f32[512,6]{0,1:T(8,128)}, f32[512,6]{0,1:T(8,128)S(1)}, u32[]{:S(2)}) copy-start(f32[512,6]{0,1:T(8,128)S(1)} %get-tuple-element.1895) | copy-start | bytes 36868
  90.3 9.3 %copy-start.44 = (f32[512,32]{0,1:T(8,128)S(1)}, f32[512,32]{0,1:T(8,128)}, u32[]{:S(2)}) copy-start(f32[512,32]{0,1:T(8,128)} %get-tuple-element.1950) | copy-start | bytes 196612
  90.3 9.3 %copy-start.46 = (f32[512,32]{0,1:T(8,128)S(1)}, f32[512,32]{0,1:T(8,128)}, u32[]{:S(2)}) copy-start(f32[512,32]{0,1:T(8,128)} %get-tuple-element.1951) | copy-start | bytes 196612
  91.8 22.6 %copy-start.8 = (f32[512,768]{0,1:T(8,128)}, f32[512,768]{0,1:T(8,128)S(1)}, u32[]{:S(2)}) copy-start(f32[512,768]{0,1:T(8,128)S(1)} %slice.261) | copy-start | bytes 4718596
  101.8 12.1 %copy-start.61 = (f32[1,6,4,128]{3,2,1,0:T(4,128)S(1)}, f32[1,6,4,128]{3,2,1,0:T(4,128)}, u32[]{:S(2)}) copy-start(f32[1,6,4,128]{3,2,1,0:T(4,128)} %copy-done.60) | copy-start | bytes 36868
  101.8 12.1 %copy-start.86 = (f32[6]{0:T(128)S(1)}, f32[6]{0:T(128)}, u32[]{:S(2)}) copy-start(f32[6]{0:T(128)} %slice_reduce_fusion) | copy-start | bytes 76
  104.5 8.8 %copy-start.80 = (f32[2,512]{1,0:T(2,128)}, f32[2,512]{1,0:T(2,128)S(1)}, u32[]{:S(2)}) copy-start(f32[2,512]{1,0:T(2,128)S(1)} %get-tuple-element.2930) | copy-start | bytes 12292
  104.5 9.9 %copy-start.31 = (bf16[1024,64]{0,1:T(8,128)(2,1)}, bf16[1024,64]{0,1:T(8,128)(2,1)S(1)}, u32[]{:S(2)}) copy-start(bf16[1024,64]{0,1:T(8,128)(2,1)S(1)} %get-tuple-element.2919) | copy-start | bytes 393220
  104.5 19.3 %copy-start.18 = (bf16[512,2,64]{0,2,1:T(8,128)(2,1)}, bf16[512,2,64]{0,2,1:T(8,128)(2,1)S(1)}, u32[]{:S(2)}) copy-start(bf16[512,2,64]{0,2,1:T(8,128)(2,1)S(1)} %get-tuple-element.2915) | copy-start | bytes 393220
  104.6 19.8 %copy-start.25 = (f32[512,2,64]{0,2,1:T(8,128)}, f32[512,2,64]{0,2,1:T(8,128)S(1)}, u32[]{:S(2)}) copy-start(f32[512,2,64]{0,2,1:T(8,128)S(1)} %get-tuple-element.1029) | copy-start | bytes 786436
  193.4 38.8 %copy-start.64 = (f32[1024,1]{0,1:T(1,128)S(1)}, f32[1024,1]{0,1:T(1,128)}, u32[]{:S(2)}) copy-start(f32[1024,1]{0,1:T(1,128)} %get-tuple-element.1922) | copy-start | bytes 12292
  193.4 99.0 %all-reduce.9.cloned.1.call-start = ((), (), s32[]{:S(2)}) async-start(), calls=%async_computation.5 | async-start | bytes 4194304 | tf_op jit(solution)/shard_map/psum | solution.py:327
  232.2 63.7 %copy-start.72 = (f32[512]{0:T(512)}, f32[512]{0:T(512)S(1)}, u32[]{:S(2)}) copy-start(f32[512]{0:T(512)S(1)} %get-tuple-element.1955) | copy-start | bytes 6148
  240.5 303.1 %all-reduce.11.cloned.1.call-start = ((), (), s32[]{:S(2)}) async-start(), calls=%async_computation.6 | async-start | bytes 3145728 | tf_op jit(solution)/shard_map/psum | solution.py:433
  305.0 17.1 %copy-start.10 = (f32[512,2,64]{0,2,1:T(8,128)}, f32[512,2,64]{0,2,1:T(8,128)S(1)}, u32[]{:S(2)}) copy-start(f32[512,2,64]{0,2,1:T(8,128)S(1)} %get-tuple-element.1048) | copy-start | bytes 786436
  322.1 8.8 %copy-start.15 = (f32[512,384]{0,1:T(8,128)}, f32[512,384]{0,1:T(8,128)S(1)}, u32[]{:S(2)}) copy-start(f32[512,384]{0,1:T(8,128)S(1)} %slice.282) | copy-start | bytes 2359300
  408.5 8.1 %copy-start.88 = (f32[2,256,256,6]{2,1,3,0:T(8,128)S(1)}, f32[2,256,256,6]{2,1,3,0:T(8,128)}, u32[]{:S(2)}) copy-start(f32[2,256,256,6]{2,1,3,0:T(8,128)} %get-tuple-element.2884) | copy-start | bytes 9437188 | tf_op jit(solution)/shard_map/transpose(jvp())/while
  499.7 144.4 %reduce-scatter.7.cloned.1.call-start = ((), (), s32[]{:S(2)}) async-start(), calls=%async_computation.7 | async-start | bytes 3538944
  569.5 169.0 %reduce-scatter.9.cloned.1.call-start = ((), (), s32[]{:S(2)}) async-start(), calls=%async_computation.8 | async-start | bytes 5013504
  (80 other events, 245.2 us)
Sparse Core Ops, SparseCore 0:
  15.4 62.8 all-gather.6
  80.9 75.4 all-gather.8
  193.6 36.8 all-reduce.6
  240.6 51.7 all-reduce.8
  499.8 43.8 all-reduce.10
  569.6 74.4 reduce-scatter.6
  647.7 90.7 reduce-scatter.8

commit v2 on v1

--- a/solution.py
+++ b/solution.py
@@ -1,6 +1,8 @@
 import jax
 import jax.numpy as jnp
 from jax import lax
+from jax.experimental import pallas as pl
+from jax.experimental.pallas import tpu as pltpu
 from jax.sharding import PartitionSpec as P
 
 MDIM = 64
@@ -17,27 +19,125 @@
 exact_dots = lax.Precision.HIGHEST
 
 
-def carried_in(shard, axis, join, neutral, backward):
-    count = lax.axis_size(axis)
-    place = lax.axis_index(axis)
-    ahead = count - 1 - place if backward else place
-    gathered = jax.tree.map(
-        lambda a, kind: lax.all_gather(a.astype(kind), axis), shard, (jnp.bfloat16, jnp.bfloat16)
-    )
-    state = jax.tree.map(lambda a, e: jnp.zeros_like(a) + jnp.asarray(e, a.dtype), shard, neutral)
-
-    def one(turn, state):
-        source = count - 1 - turn if backward else turn
-        return join(
-            state,
-            jax.tree.map(
-                lambda a, own: lax.dynamic_index_in_dim(a, source, 0, False).astype(own.dtype),
-                gathered,
-                shard,
-            ),
-        )
-
-    return lax.fori_loop(0, ahead, one, state)
+def across(left, right):
+    return lax.dot_general(
+        left, right, (((1,), (1,)), ((), ())), preferred_element_type=jnp.float32
+    )
+
+
+def over_rows(left, right):
+    return lax.dot_general(
+        left, right, (((0,), (0,)), ((), ())), preferred_element_type=jnp.float32
+    )
+
+
+def mixer_forward(gate, inputs, b_part, c_part, step, cum_col, cum_row, skip, state, gated, mixer_y):
+    rows = inputs.shape[0]
+    b_b = b_part[...].astype(jnp.bfloat16)
+    c_b = c_part[...].astype(jnp.bfloat16)
+    products = across(c_b, b_b)
+    carried = across(c_b, state[...].astype(jnp.bfloat16))
+    lower = lax.broadcasted_iota(jnp.int32, (rows, rows), 0) >= lax.broadcasted_iota(
+        jnp.int32, (rows, rows), 1
+    )
+    for head in range(step.shape[1]):
+        cols = slice(head * MDIM, (head + 1) * MDIM)
+        column = cum_col[:, head : head + 1]
+        decays = jnp.exp(jnp.where(lower, column - cum_row[head : head + 1, :], NEG_FILL))
+        weights_b = (products * decays).astype(jnp.bfloat16)
+        part = inputs[:, cols]
+        driven_b = (part * step[:, head : head + 1]).astype(jnp.bfloat16)
+        y_part = (
+            jnp.dot(weights_b, driven_b, preferred_element_type=jnp.float32)
+            + carried[:, cols] * jnp.exp(column)
+            + skip[:, cols] * part
+        )
+        gate_part = gate[:, cols]
+        mixer_y[:, cols] = y_part
+        gated[:, cols] = (y_part * gate_part * jax.nn.sigmoid(gate_part)).astype(jnp.bfloat16)
+
+
+def mixer_backward(
+    dgated, gate, inputs, mixer_y, b_part, c_part, step, cum_col, cum_row, skip, state, later,
+    dmix, dshared, decay_col, decay_row, dstep, dskip,
+):
+    rows = inputs.shape[0]
+    inner = inputs.shape[1]
+    b_b = b_part[...].astype(jnp.bfloat16)
+    c_b = c_part[...].astype(jnp.bfloat16)
+    state_b = state[...].astype(jnp.bfloat16)
+    later_b = later[...].astype(jnp.bfloat16)
+    products = across(c_b, b_b)
+    carried = across(c_b, state_b)
+    later_rows = across(b_b, later_b)
+    lower = lax.broadcasted_iota(jnp.int32, (rows, rows), 0) >= lax.broadcasted_iota(
+        jnp.int32, (rows, rows), 1
+    )
+    dproducts = jnp.zeros((rows, rows), jnp.float32)
+    db_total = jnp.zeros(b_part.shape, jnp.float32)
+    dc_total = jnp.zeros(c_part.shape, jnp.float32)
+    last_row = lax.broadcasted_iota(jnp.int32, (rows, 1), 0) == rows - 1
+    for head in range(step.shape[1]):
+        cols = slice(head * MDIM, (head + 1) * MDIM)
+        column = cum_col[:, head : head + 1]
+        decays = jnp.exp(jnp.where(lower, column - cum_row[head : head + 1, :], NEG_FILL))
+        weights = products * decays
+        part = inputs[:, cols]
+        step_part = step[:, head : head + 1]
+        driven = part * step_part
+        gate_part = gate[:, cols]
+        sigmoid = jax.nn.sigmoid(gate_part)
+        dgated_part = dgated[:, cols]
+        dy = dgated_part * gate_part * sigmoid
+        dgate = dgated_part * mixer_y[:, cols] * sigmoid * (1.0 + gate_part * (1.0 - sigmoid))
+        dy_b = dy.astype(jnp.bfloat16)
+        growth = jnp.exp(column)
+        tail = jnp.exp(cum_col[rows - 1 : rows, head : head + 1] - column)
+        later_part = tail * later_rows[:, cols]
+        ddriven = over_rows(weights.astype(jnp.bfloat16), dy_b) + later_part
+        dweights = across(dy_b, driven.astype(jnp.bfloat16))
+        dproducts = dproducts + dweights * decays
+        pulls = dweights * weights
+        tail_pull = jnp.sum(driven * later_part, axis=1, keepdims=True)
+        total = (
+            jnp.sum(pulls, axis=1, keepdims=True)
+            + growth * jnp.sum(dy * carried[:, cols], axis=1, keepdims=True)
+            - tail_pull
+        )
+        total = total + jnp.where(last_row, jnp.sum(tail_pull, axis=0, keepdims=True), 0.0)
+        decay_col[:, head : head + 1] = total
+        decay_row[head : head + 1, :] = jnp.sum(pulls, axis=0, keepdims=True)
+        dc_total = dc_total + jnp.dot(
+            (growth * dy).astype(jnp.bfloat16),
+            state_b[cols, :],
+            preferred_element_type=jnp.float32,
+        )
+        db_total = db_total + jnp.dot(
+            (tail * driven).astype(jnp.bfloat16),
+            later_b[cols, :],
+            preferred_element_type=jnp.float32,
+        )
+        dstep[:, head : head + 1] = jnp.sum(ddriven * part, axis=1, keepdims=True)
+        dskip[:, cols] = jnp.sum(dy * part, axis=0, keepdims=True)
+        dmix[:, cols] = dgate.astype(jnp.bfloat16)
+        dmix[:, inner + head * MDIM : inner + (head + 1) * MDIM] = (
+            ddriven * step_part + skip[:, cols] * dy
+        ).astype(jnp.bfloat16)
+    dproducts_b = dproducts.astype(jnp.bfloat16)
+    width = b_part.shape[1]
+    dshared[:, :width] = (db_total + over_rows(dproducts_b, c_b)).astype(jnp.bfloat16)
+    dshared[:, width:] = (
+        dc_total + jnp.dot(dproducts_b, b_b, preferred_element_type=jnp.float32)
+    ).astype(jnp.bfloat16)
+
+
+def on_core(body, results, cost):
+    return pl.pallas_call(
+        body,
+        out_shape=results,
+        compiler_params=pltpu.CompilerParams(vmem_limit_bytes=48 * 1024 * 1024),
+        cost_estimate=pl.CostEstimate(flops=cost, bytes_accessed=8_000_000, transcendentals=0),
+    )
 
 
 def angle_tables(places, width):
@@ -65,57 +165,6 @@
         [first_half * cosine + second * sine_part, second * cosine - first_half * sine_part],
         axis=-1,
     )
-
-
-def step_decay(step_raw, inputs, step_bias, decay_log, live_mask):
-    step_size = jax.nn.softplus(step_raw + step_bias[None, :]) * live_mask[:, None]
-    log_decay = -jnp.exp(decay_log)[None, :] * step_size
-    driven = inputs * step_size[:, :, None]
-    return (log_decay, driven)
-
-
-def state_space(
-    inputs, gate_pre, b_proj, c_proj, step_raw, step_bias, decay_log, skip_gain, live_mask, state_in
-):
-    row_count, head_count, head_width = inputs.shape
-    log_decay, driven = step_decay(step_raw, inputs, step_bias, decay_log, live_mask)
-    block_count = row_count // STRETCH
-    lower = jnp.arange(STRETCH)[:, None] >= jnp.arange(STRETCH)[None, :]
-
-    def advance(state, pieces):
-        decay_part, driven_part, b_part, c_part, input_part = pieces
-        cumulative = jnp.cumsum(decay_part, axis=0)
-        differences = cumulative[:, None, :] - cumulative[None, :, :]
-        decays = jnp.exp(jnp.where(lower[:, :, None], differences, NEG_FILL))
-        products = jnp.dot(c_part, b_part.T, precision=exact_dots)
-        within = jnp.einsum("ts,tsh,shp->thp", products, decays, driven_part, precision=exact_dots)
-        carried = (
-            jnp.einsum("tn,hnp->thp", c_part, state, precision=exact_dots)
-            * jnp.exp(cumulative)[:, :, None]
-        )
-        tail_decay = jnp.exp(cumulative[-1][None, :] - cumulative)
-        new_state = jnp.exp(cumulative[-1])[:, None, None] * state + jnp.einsum(
-            "sh,sn,shp->hnp", tail_decay, b_part, driven_part, precision=exact_dots
-        )
-        return (new_state, within + carried + skip_gain[None, :, None] * input_part)
-
-    state_out, outputs = lax.scan(
-        advance,
-        state_in,
-        (
-            log_decay.reshape(block_count, STRETCH, head_count),
-            driven.reshape(block_count, STRETCH, head_count, head_width),
-            b_proj.reshape(block_count, STRETCH, -1),
-            c_proj.reshape(block_count, STRETCH, -1),
-            inputs.reshape(block_count, STRETCH, head_count, head_width),
-        ),
-    )
-    mixer_y = outputs.reshape(row_count, head_count, head_width)
-    return (mixer_y * jax.nn.silu(gate_pre), state_out)
-
-
-def chain_states(earlier, later):
-    return (earlier[0] * later[0], later[0][:, None, None] * earlier[1] + later[1])
 
 
 def per_device(
@@ -186,9 +235,8 @@
     inv_one = lax.rsqrt(jnp.mean(inputs_f * inputs_f, axis=-1, keepdims=True) + EPS)
     normed = (inputs_f * inv_one * gain_in.astype(jnp.float32)).astype(jnp.bfloat16)
     all_cols = jnp.dot(normed, full_in[:, :step_end], preferred_element_type=jnp.float32)
-    projected = all_cols[:, :mix_end].reshape(row_count, 2, heads_here, MDIM)
-    gate_pre = projected[:, 0]
-    inputs = projected[:, 1]
+    gate_pre = all_cols[:, :inner_here]
+    inputs = all_cols[:, inner_here:mix_end]
     step_raw = all_cols[:, query_end:]
     b_proj = all_cols[:, mix_end : mix_end + STATE]
     c_proj = all_cols[:, mix_end + STATE : state_end]
@@ -200,61 +248,53 @@
     query_b = rotate(queries, places).astype(jnp.bfloat16)
     key_b = rotate(key_raw[:, None, :], places)[:, 0].astype(jnp.bfloat16)
     own_keyval = jnp.concatenate([key_b, value_raw.astype(jnp.bfloat16)], axis=1)
-    all_keyval = lax.all_gather(own_keyval, "ctx", axis=0, tiled=True)
+    step_size = jax.nn.softplus(step_raw + step_bias[None, :]) * live_mask[:, None]
+    log_decay = -jnp.exp(decay_log)[None, :] * step_size
+    row_places = jnp.arange(row_count)
+    below = (row_places[:, None] >= row_places[None, :]).astype(jnp.float32)
+    cumulative = jnp.cumsum(log_decay, axis=0)
+    cum_row = cumulative.T
+    head_wide = lambda values: jnp.repeat(values, MDIM, axis=-1)
+    tail_step = jnp.exp(cumulative[-1][None, :] - cumulative) * step_size
+    own_state = jnp.dot(
+        (inputs * head_wide(tail_step)).astype(jnp.bfloat16).T,
+        b_proj.astype(jnp.bfloat16),
+        preferred_element_type=jnp.float32,
+    )
+    own_decay = jnp.pad(jnp.exp(cumulative[-1]), (0, STATE - heads_here))
+    sent = jnp.concatenate(
+        [
+            own_keyval,
+            own_state.astype(jnp.bfloat16),
+            jnp.broadcast_to(own_decay[None, :], (16, STATE)).astype(jnp.bfloat16),
+        ],
+        axis=0,
+    )
+    received = lax.all_gather(sent, "ctx", axis=0)
+    all_keyval = received[:, :row_count].reshape(-1, 2 * HDIM)
     all_keys = all_keyval[:, :HDIM]
     values = all_keyval[:, HDIM:]
-    log_decay, driven = step_decay(step_raw, inputs, step_bias, decay_log, live_mask)
-    cumulative = jnp.cumsum(log_decay, axis=0)
-    own_decay = jnp.exp(cumulative[-1])
-    own_state = jnp.einsum(
-        "sh,sn,shp->hnp",
-        jnp.exp(cumulative[-1][None, :] - cumulative),
-        b_proj,
-        driven,
-        precision=exact_dots,
-    )
-    identity = (jnp.ones_like(own_decay), jnp.zeros_like(own_state))
-    decay_before, state_in = carried_in(
-        (own_decay, own_state), "ctx", chain_states, identity, False
-    )
-
-    def mixer_fn(
-        input_part,
-        gate_part,
-        b_part,
-        c_part,
-        step_part,
-        bias_part,
-        decay_part,
-        skip_part,
-        state_part,
-    ):
-        return state_space(
-            input_part,
-            gate_part,
-            b_part,
-            c_part,
-            step_part,
-            bias_part,
-            decay_part,
-            skip_part,
-            live_mask,
-            state_part,
-        )
-
-    (gated, state_last), mixer_back = jax.vjp(
-        mixer_fn,
-        inputs,
-        gate_pre,
-        b_proj,
-        c_proj,
-        step_raw,
-        step_bias,
-        decay_log,
-        skip_gain,
-        state_in,
-    )
-    gated_b = gated.astype(jnp.bfloat16).reshape(row_count, inner_here)
+    state_stop_row = row_count + inner_here
+    ctx_count = received.shape[0]
+    all_states = received[:, row_count:state_stop_row].astype(jnp.float32)
+    all_decays = head_wide(
+        received[:, state_stop_row, :heads_here].astype(jnp.float32)
+    )[:, :, None]
+    state_in = jnp.zeros((inner_here, STATE), jnp.float32)
+    for source in range(ctx_count - 1):
+        state_in = jnp.where(
+            source < ctx_index, all_decays[source] * state_in + all_states[source], state_in
+        )
+    skip_wide = head_wide(skip_gain)[None, :]
+    quadratic = row_count * row_count * inner_here
+    gated_b, mixer_y = on_core(
+        mixer_forward,
+        (
+            jax.ShapeDtypeStruct((row_count, inner_here), jnp.bfloat16),
+            jax.ShapeDtypeStruct((row_count, inner_here), jnp.float32),
+        ),
+        20 * quadratic,
+    )(gate_pre, inputs, b_proj, c_proj, step_size, cumulative, cum_row, skip_wide, state_in)
     block_rows = min(512, row_count)
     score_scale = HDIM ** (-0.5)
     block_count = (ctx_index + 1) * (row_count // block_rows)
@@ -340,29 +380,21 @@
     mixers_grad_t = jnp.dot(dmixed_b.T, mixers_b, preferred_element_type=jnp.float32)
     out_rows = lax.psum_scatter(
         jnp.concatenate(
-            [mixers_grad_t, down_grad_t, gate_up_grad, ffn_norm_grad[:, None]], axis=1
-        ).astype(jnp.bfloat16),
+            [
+                mixers_grad_t.astype(jnp.bfloat16),
+                down_grad_t.astype(jnp.bfloat16),
+                gate_up_grad.astype(jnp.bfloat16),
+            ],
+            axis=1,
+        ),
         ("fsdp", "ctx"),
         scatter_dimension=0,
         tiled=True,
-    ).astype(jnp.float32)
+    )
     dmixers = jnp.dot(dmixed_b, full_mixers_t, preferred_element_type=jnp.float32)
-    dgated = dmixers[:, :inner_here].reshape(row_count, heads_here, MDIM)
+    dgated = dmixers[:, :inner_here]
     dattended_b = (
         dmixers[:, inner_here:].reshape(row_count, query_here, HDIM).astype(jnp.bfloat16)
-    )
-    dstate_direct = jnp.einsum(
-        "sn,sh,shp->hnp",
-        c_proj,
-        jnp.exp(cumulative),
-        dgated * jax.nn.silu(gate_pre),
-        precision=exact_dots,
-    )
-    decay_after, later_grad = carried_in(
-        (own_decay, dstate_direct), "ctx", chain_states, identity, True
-    )
-    dinputs, dgate_pre, db_proj, dc_proj, dstep_raw, dbias, ddecay, dskip, dstate_unused = (
-        mixer_back((dgated, later_grad))
     )
     row_terms = jnp.sum(dattended_b.astype(jnp.float32) * attended_b.astype(jnp.float32), axis=-1).T
 
@@ -403,13 +435,62 @@
             jnp.zeros((all_keyval.shape[0], 2 * HDIM), jnp.float32),
         ),
     )
-    all_dkeyval = lax.all_gather(dkeyval.astype(jnp.bfloat16), "ctx", axis=0)
+    dstate_direct = jnp.dot(
+        (dgated * jax.nn.silu(gate_pre) * head_wide(jnp.exp(cumulative))).astype(jnp.bfloat16).T,
+        c_proj.astype(jnp.bfloat16),
+        preferred_element_type=jnp.float32,
+    )
+    keyval_rows_all = dkeyval.shape[0]
+    returned = lax.all_gather(
+        jnp.concatenate([dkeyval, dstate_direct], axis=0).astype(jnp.bfloat16), "ctx", axis=0
+    )
     own_dkeyval = jnp.sum(
-        lax.dynamic_slice_in_dim(all_dkeyval, ctx_index * row_count, row_count, 1).astype(
+        lax.dynamic_slice_in_dim(returned, ctx_index * row_count, row_count, 1).astype(
             jnp.float32
         ),
         axis=0,
     )
+    all_dstates = returned[:, keyval_rows_all:].astype(jnp.float32)
+    later_grad = jnp.zeros((inner_here, STATE), jnp.float32)
+    for source in range(ctx_count - 1, 0, -1):
+        later_grad = jnp.where(
+            source > ctx_index, all_decays[source] * later_grad + all_dstates[source], later_grad
+        )
+    dmix_in_b, dstate_b, decay_col, decay_row, dstep_direct, dskip_wide = on_core(
+        mixer_backward,
+        (
+            jax.ShapeDtypeStruct((row_count, 2 * inner_here), jnp.bfloat16),
+            jax.ShapeDtypeStruct((row_count, 2 * STATE), jnp.bfloat16),
+            jax.ShapeDtypeStruct((row_count, heads_here), jnp.float32),
+            jax.ShapeDtypeStruct((heads_here, row_count), jnp.float32),
+            jax.ShapeDtypeStruct((row_count, heads_here), jnp.float32),
+            jax.ShapeDtypeStruct((1, inner_here), jnp.float32),
+        ),
+        60 * quadratic,
+    )(
+        dgated,
+        gate_pre,
+        inputs,
+        mixer_y,
+        b_proj,
+        c_proj,
+        step_size,
+        cumulative,
+        cum_row,
+        skip_wide,
+        state_in,
+        later_grad,
+    )
+    through_state = jnp.exp(cumulative[-1]) * jnp.sum(
+        (state_in * later_grad).reshape(heads_here, -1), axis=1
+    )
+    dcumulative = decay_col - decay_row.T
+    dlog_decay = jnp.dot(below.T, dcumulative, precision=exact_dots) + through_state[None, :]
+    dstep_size = dstep_direct - jnp.exp(decay_log)[None, :] * dlog_decay
+    dstep_raw = dstep_size * live_mask[:, None] * jax.nn.sigmoid(step_raw + step_bias[None, :])
+    dbias = jnp.sum(dstep_raw, axis=0)
+    ddecay = jnp.sum(dlog_decay * log_decay, axis=0)
+    dskip = jnp.sum(dskip_wide.reshape(heads_here, MDIM), axis=1)
     dkey_rot = rotate_back(own_dkeyval[:, None, :HDIM], places)[:, 0]
     dkeyval_full = jnp.zeros((row_count, 2 * kv_span), jnp.float32)
     dkeyval_full = lax.dynamic_update_slice_in_dim(dkeyval_full, dkey_rot, kv_head * HDIM, 1)
@@ -420,27 +501,25 @@
     dquery_b = (
         rotate_back(dquery, places).reshape(row_count, query_here * HDIM).astype(jnp.bfloat16)
     )
-    dstate_b = jnp.concatenate([db_proj, dc_proj], axis=1).astype(jnp.bfloat16)
-    dmix_in_b = (
-        jnp.stack([dgate_pre, dinputs], axis=1)
-        .reshape(row_count, 2 * inner_here)
-        .astype(jnp.bfloat16)
-    )
     dstep_b = dstep_raw.astype(jnp.bfloat16)
     shared_b = jnp.concatenate([dstate_b, dkeyval_b], axis=1)
     dcols_b = jnp.concatenate([dmix_in_b, shared_b, dquery_b, dstep_b], axis=1)
     group_term = jnp.dot(dcols_b, full_in[:, :step_end].T, preferred_element_type=jnp.float32)
+    group_term, out_rows = lax.optimization_barrier((group_term, out_rows))
+    out_rows = out_rows.astype(jnp.float32)
     group_sums = lax.psum(
         jnp.concatenate([group_term.astype(jnp.bfloat16), shared_b], axis=1), "tp"
     )
     dnormed = group_sums[:, :width_model].astype(jnp.float32)
     shared_sum = group_sums[:, width_model:]
-    own_grad = jnp.dot(
+    packed_cols = [dmix_in_b, dquery_b, shared_sum, dstep_b]
+    used = step_end
+    spare = -(used + 5) % 128 + 5
+    grads_in = jnp.dot(
         normed.T,
-        jnp.concatenate([dmix_in_b, dquery_b, dstep_b], axis=1),
+        jnp.concatenate(packed_cols + [jnp.zeros((row_count, spare), jnp.bfloat16)], axis=1),
         preferred_element_type=jnp.float32,
     )
-    shared_grad = jnp.dot(normed.T, shared_sum, preferred_element_type=jnp.float32)
     scaled_one = gain_in.astype(jnp.float32) * dnormed
     in_norm_grad = jnp.sum(dnormed * inputs_f * inv_one, axis=0)
     input_grad = (
@@ -452,33 +531,35 @@
         jnp.pad(jnp.stack([dbias, ddecay, dskip], axis=1), ((0, shard_rows - heads_here), (0, 0))),
         (width_model // shard_rows, 1),
     )
+    slot = jnp.arange(used + spare)[None, :] - used
+    extra = jnp.where(slot == 0, in_norm_grad[:, None], 0.0)
+    extra = jnp.where(slot == 1, ffn_norm_grad[:, None], extra)
+    for column in range(3):
+        extra = jnp.where(slot == 2 + column, head_columns[:, column : column + 1], extra)
     in_rows = lax.psum_scatter(
-        jnp.concatenate(
-            [own_grad, shared_grad, in_norm_grad[:, None], head_columns], axis=1
-        ).astype(jnp.bfloat16),
+        (grads_in + extra).astype(jnp.bfloat16),
         ("fsdp", "ctx"),
         scatter_dimension=0,
         tiled=True,
     ).astype(jnp.float32)
     query_stop = mix_end + query_cols
-    step_stop = query_stop + heads_here
-    state_stop = step_stop + state_span
+    state_stop = query_stop + state_span
     keyval_stop = state_stop + keyval_span
     mixer_in_rows = in_rows[:, :mix_end].reshape(shard_rows, 2, inner_here)
     query_rows = in_rows[:, mix_end:query_stop]
-    step_rows = in_rows[:, query_stop:step_stop]
-    state_rows = in_rows[:, step_stop:state_stop]
+    step_rows = in_rows[:, keyval_stop:used]
+    state_rows = in_rows[:, query_stop:state_stop]
     keyval_rows = in_rows[:, state_stop:keyval_stop]
-    in_norm_rows = in_rows[:, keyval_stop]
-    bias_grad = in_rows[:heads_here, keyval_stop + 1]
-    decay_grad = in_rows[:heads_here, keyval_stop + 2]
-    skip_grad = in_rows[:heads_here, keyval_stop + 3]
+    in_norm_rows = in_rows[:, used]
+    ffn_norm_rows = in_rows[:, used + 1]
+    bias_grad = in_rows[:heads_here, used + 2]
+    decay_grad = in_rows[:heads_here, used + 3]
+    skip_grad = in_rows[:heads_here, used + 4]
     mixer_out_rows = out_rows[:, :inner_here].T
     attn_out_rows = out_rows[:, inner_here:attn_end].T
     down_rows = out_rows[:, attn_end:down_end].T
     gate_rows = out_rows[:, down_end:gate_end]
     up_rows = out_rows[:, gate_end : gate_end + hidden_here]
-    ffn_norm_rows = out_rows[:, gate_end + hidden_here]
     return (
         block_out[None],
         input_grad[None],

time: 764 us -> 517 us (0.68)
  local copies, waits for them, and re-layouts: 198 us -> 70.3 us
  other arithmetic: 93.1 us -> 46 us
  waiting for transfers between devices: 327 us -> 289 us
  matrix products: 75 us -> 43 us
  Pallas kernels: 0 us -> 12.4 us
    unnamed x9 -> x8, waiting for transfers between devices: 145 us -> 19.7 us
    dynamic_update_slice x32 -> x2, local copies, waits for them, and re-layouts: 66.6 us -> 3.23 us  [back_block(): lax.dynamic_update_slice_in_dim(dkeyval, jnp.concatenate([dkey_part, dval...]
    reduce_scatter x0 -> x1, waiting for transfers between devices: none -> 60 us  [per_device(): lax.psum_scatter((grads_in + extra).astype(jnp.bfloat16), ('fsdp', 'ctx')...]
    dot_general x26 -> x4, matrix products: 47.2 us -> 9.37 us  [the longest x1 4.44 us: per_device(): jnp.dot(normed.T, jnp.concatenate(packed_cols + [jnp.zeros((row_count, sp...]
    all_gather x1, waiting for transfers between devices: 0.01 us -> 33.8 us  [per_device(): full_out = lax.all_gather(weights_out, ('fsdp', 'ctx'), axis=0, tiled=True)]
    another operation x27 -> x6, other arithmetic: 32.5 us -> 6.28 us
    another operation x37 -> x6, local copies, waits for them, and re-layouts: 20.3 us -> 1.08 us
    concatenate x1, local copies, waits for them, and re-layouts: 16.1 us -> 1.99 us  [per_device(): jnp.concatenate(packed_cols + [jnp.zeros((row_count, spare), jnp.bfloat16...]
  transfers between devices with their start and end apart: 7 -> 7, of which waited for: 6 -> 7; matrix products, arithmetic and copies ran while one was open for 16% -> 16% of each run, Pallas kernels for 0% -> 2%
where the time goes in v2:
time: 517 us; the launch traced here: 510 us
  waiting for transfers between devices  289 us (56%)
  local copies, waits for them, and re-layouts  70.3 us (14%)
  other arithmetic  46 us (9%)
  matrix products  43 us (8%)
  blocking collectives  32.5 us (6%)
  between operations  16.2 us (3%)
  Pallas kernels  12.4 us (2%)
    reduce_scatter x1, waiting for transfers between devices, per_device(): lax.psum_scatter((grads_in + extra).astype(jnp.bfloat16), ('fsdp', 'ctx')...  60 us
    all_gather x1, waiting for transfers between devices, per_device(): full_in = lax.all_gather(weights_in, ('fsdp', 'ctx'), axis=0, tiled=True)  57.6 us
    psum x1, waiting for transfers between devices, per_device(): lax.psum(jnp.concatenate([group_term.astype(jnp.bfloat16), shared_b], axi...  42.4 us
    psum x1, waiting for transfers between devices, per_device(): lax.psum(jnp.concatenate([dnormed_two_term, ffn_term], axis=1).astype(jnp...  41.3 us
    psum x1, waiting for transfers between devices, per_device(): lax.psum(partial_term.astype(jnp.bfloat16), 'tp').astype(jnp.float32)  34.4 us
    all_gather x1, waiting for transfers between devices, per_device(): full_out = lax.all_gather(weights_out, ('fsdp', 'ctx'), axis=0, tiled=True)  33.8 us
    unnamed x147, local copies, waits for them, and re-layouts  28.8 us
    all_gather x1, blocking collectives, per_device(): lax.all_gather(jnp.concatenate([dkeyval, dstate_direct], axis=0).astype(j...  24 us
  transfers between devices with their start and end apart: 7, of which 7 were waited for; matrix products, arithmetic and copies ran while one was open for 16% of the time, Pallas kernels for 2%

profile of v2, /device:TPU:0, one launch (start us, length us, event | category | flops | bytes accessed | tf_op | source)
XLA Modules:
  0.0 510.2 jit_solution(15032700510406639727)
XLA Ops:
  11.4 3.9 concatenate.70
  20.8 57.6 %all-gather.4.cloned.1.call-done = bf16[1024,1416]{0,1:T(8,128)(2,1)} async-done(((bf16[128,1416]{0,1:T(8,128)(2,1)}), bf16[1024,1416]{0,1:T(8,128)(2,1)}) %all-gather.4.cloned.1.call-update) | async-done | bytes 2899984 | tf_op jit(solution)/shard_map/all_gather | solution.py:210
  79.2 3.6 fusion.50
  94.3 8.6 %all-gather = bf16[1824,128]{1,0:T(8,128)(2,1)S(1)} all-gather(bf16[912,128]{1,0:T(8,128)(2,1)S(1)} %pad_maximum_fusion.11), channel_id=2, replica_groups=mesh['fsdp'=4,'ctx'=2,'tp'=4] {'ctx'}, dimensions={0}, use_global_device_ids=true | all-gather | bytes 700416 | tf_op jit(solution)/shard_map/all_gather | solution.py:273
  107.9 2.1 while.37
  110.6 2.7 while.38
  115.2 3.6 shard_map.305
  120.4 33.8 %all-gather.6.cloned.1.call-done = bf16[1024,2048]{0,1:T(8,128)(2,1)} async-done(((bf16[128,2048]{0,1:T(8,128)(2,1)}), bf16[1024,2048]{0,1:T(8,128)(2,1)}) %all-gather.6.cloned.1.call-update) | async-done | bytes 4194320 | tf_op jit(solution)/shard_map/all_gather | solution.py:211
  154.2 3.0 convolution_convert_fusion.4
  157.3 34.4 %all-reduce.6.cloned.1.call-done = bf16[512,1024]{1,0:T(8,128)(2,1)} async-done(((bf16[512,1024]{1,0:T(8,128)(2,1)}), bf16[512,1024]{1,0:T(8,128)(2,1)}) %all-reduce.6.cloned.1.call-update) | async-done | bytes 1048592 | tf_op jit(solution)/shard_map/psum | solution.py:347
  191.7 2.1 multiply_reduce_fusion.2
  193.9 3.1 fusion.66
  203.4 2.3 copy.224
  205.9 3.2 fusion.71
  209.1 3.8 convolution_convert_fusion
  212.9 41.3 %all-reduce.8.cloned.1.call-done = bf16[512,2048]{1,0:T(8,128)(2,1)} async-done(((bf16[512,2048]{1,0:T(8,128)(2,1)}), bf16[512,2048]{1,0:T(8,128)(2,1)}) %all-reduce.8.cloned.1.call-update) | async-done | bytes 2097168 | tf_op jit(solution)/shard_map/psum | solution.py:367
  254.1 2.3 convert_element_type.220
  259.6 2.7 fusion.78
  267.1 4.1 pad_maximum_fusion.1
  271.2 6.5 %copy.243 = bf16[1024,2048]{1,0:T(8,128)(2,1)} copy(bf16[1024,2048]{0,1:T(8,128)(2,1)} %pad_maximum_fusion.1) | data formatting | bytes 8388608
  277.8 2.3 fusion.72
  281.5 10.4 %while.39 = (s32[]{:T(128)}, f32[512,2,64]{0,2,1:T(8,128)}, bf16[1024,128]{1,0:T(8,128)(2,1)}, s32[]{:T(128)}, bf16[1024,64]{0,1:T(8,128)(2,1)}, /*index=5*/s32[...) while((s32[]{:T(128)}, f32[512,2,64]{0,2,1:T(8,128)}, ...), condition=%wide.region_15.16_spmd.clone, body=%wide.region_14.15_spmd.clone.sunk | while | flops 340199424 | bytes 13714743 | solution.py:429
  292.9 24.0 %all_gather.20 = bf16[2,1408,128]{2,1,0:T(8,128)(2,1)S(1)} all-gather(bf16[1,1408,128]{2,1,0:T(8,128)(2,1)S(1)} %pad_maximum_fusion.8), channel_id=1, replica_groups=mesh['fsdp'=4,'ctx'=2,'tp'=4] {'ctx'}, dimensions={0}, use_global_device_ids=true | all-gather | bytes 1081344 | tf_op jit(solution)/shard_map/all_gather | solution.py:444
  323.4 8.8 %shard_map.306 = (bf16[512,768]{1,0:T(8,128)(2,1)S(1)}, bf16[512,256]{1,0:T(8,128)(2,1)S(1)}, f32[512,6]{1,0:T(8,128)S(1)}, f32[6,512]{1,0:T(8,128)S(1)}, f32[512,6]{1,0:T(8,128)S(1)}, /*index=5*/f32[1,384]{1,0:T(1,128)S(1)}) custom-call(f32[512,384]{1,0:T(8,128)S(1)} %copy-done.1, f32[512,384]{1,0:T(8,128)S(1)} %copy.247.gate, ...), custom_call_target="tpu_custom_call" | custom-call | flops 6039797760 | bytes 8000000 | tf_op jit(solution)/shard_map/pallas_call | solution.py:459
  346.5 19.6 %reduce-scatter.7.cloned.1.call-done = bf16[128,2048]{1,0:T(8,128)(2,1)} async-done(((bf16[1024,2048]{1,0:T(8,128)(2,1)}), bf16[128,2048]{1,0:T(8,128)(2,1)}) %reduce-scatter.7.cloned.1.call-update) | async-done | bytes 524304
  366.1 2.1 copy.244
  369.8 42.4 %all-reduce.10.cloned.1.call-done = bf16[512,1536]{1,0:T(8,128)(2,1)} async-done(((bf16[512,1536]{1,0:T(8,128)(2,1)}), bf16[512,1536]{1,0:T(8,128)(2,1)}) %all-reduce.10.cloned.1.call-update) | async-done | bytes 1572880 | tf_op jit(solution)/shard_map/psum | solution.py:510
  415.4 2.2 fusion.62
  417.6 4.4 add_convert_fusion
  422.1 2.3 convert_element_type.241
  433.4 3.1 fusion.55
  436.6 60.0 %reduce-scatter.5.cloned.1.call-done = bf16[128,1536]{1,0:T(8,128)(2,1)} async-done(((bf16[1024,1536]{1,0:T(8,128)(2,1)}), bf16[128,1536]{1,0:T(8,128)(2,1)}) %reduce-scatter.5.cloned.1.call-update) | async-done | bytes 393232 | tf_op jit(solution)/shard_map/reduce_scatter | solution.py:539
  (308 shorter events, 102.8 us)
Async XLA Ops:
  7.2 9.2 %copy-start.39 = (bf16[128,512]{1,0:T(8,128)(2,1)S(1)}, bf16[128,512]{1,0:T(8,128)(2,1)}, u32[]{:S(2)}) copy-start(bf16[128,512]{1,0:T(8,128)(2,1)} %param.40) | copy-start | bytes 393220
  7.2 9.3 %copy-start.41 = (bf16[384,128]{1,0:T(8,128)(2,1)S(1)}, bf16[384,128]{1,0:T(8,128)(2,1)}, u32[]{:S(2)}) copy-start(bf16[384,128]{1,0:T(8,128)(2,1)} %param.37) | copy-start | bytes 294916
  7.2 9.3 %copy-start.42 = (bf16[128,128]{1,0:T(8,128)(2,1)S(1)}, bf16[128,128]{1,0:T(8,128)(2,1)}, u32[]{:S(2)}) copy-start(bf16[128,128]{1,0:T(8,128)(2,1)} %param.38) | copy-start | bytes 98308
  7.2 9.3 %copy-start.40 = (bf16[512,128]{1,0:T(8,128)(2,1)S(1)}, bf16[512,128]{1,0:T(8,128)(2,1)}, u32[]{:S(2)}) copy-start(bf16[512,128]{1,0:T(8,128)(2,1)} %param.41) | copy-start | bytes 393220
  7.2 10.4 %copy-start.10 = (bf16[1,512,1024]{2,1,0:T(8,128)(2,1)S(1)}, bf16[1,512,1024]{2,1,0:T(8,128)(2,1)}, u32[]{:S(2)}) copy-start(bf16[1,512,1024]{2,1,0:T(8,128)(2,1)} %param.24) | copy-start | bytes 3145732
  7.2 71.1 %all-gather.4.cloned.1.call-start = ((), (), s32[]{:S(2)}) async-start(), calls=%async_computation.2 | async-start | bytes 3262464 | tf_op jit(solution)/shard_map/all_gather | solution.py:210
  11.3 7.8 %copy-start.56 = (f32[6]{0:T(128)S(1)}, f32[6]{0:T(128)}, u32[]{:S(2)}) copy-start(f32[6]{0:T(128)} %param.35) | copy-start | bytes 76
  11.3 8.4 %copy-start.54 = (f32[6]{0:T(128)S(1)}, f32[6]{0:T(128)}, u32[]{:S(2)}) copy-start(f32[6]{0:T(128)} %param.36) | copy-start | bytes 76
  15.3 138.9 %all-gather.6.cloned.1.call-start = ((), (), s32[]{:S(2)}) async-start(), calls=%async_computation.3 | async-start | bytes 4718592 | tf_op jit(solution)/shard_map/all_gather | solution.py:211
  17.5 174.2 %all-reduce.6.cloned.1.call-start = ((), (), s32[]{:S(2)}) async-start(), calls=%async_computation.4 | async-start | bytes 2097152 | tf_op jit(solution)/shard_map/psum | solution.py:347
  17.5 70.6 %copy-start.47 = (f32[32]{0:T(128)}, f32[32]{0:T(128)S(1)}, u32[]{:S(2)}) copy-start(f32[32]{0:T(128)S(1)} %negate_power_fusion) | copy-start | bytes 388
  18.5 64.3 %copy-start.43 = (f32[512]{0:T(512)}, f32[512]{0:T(512)S(1)}, u32[]{:S(2)}) copy-start(f32[512]{0:T(512)S(1)} %get-tuple-element.489) | copy-start | bytes 6148
  19.2 64.8 %copy-start.46 = (f32[512]{0:T(512)}, f32[512]{0:T(512)S(1)}, u32[]{:S(2)}) copy-start(f32[512]{0:T(512)S(1)} %fusion.117) | copy-start | bytes 6148
  19.7 64.3 %copy-start.53 = (f32[6]{0:T(128)}, f32[6]{0:T(128)S(1)}, u32[]{:S(2)}) copy-start(f32[6]{0:T(128)S(1)} %get-tuple-element.495) | copy-start | bytes 76
  92.5 11.8 %copy-start.32 = (f32[512,128]{0,1:T(8,128)S(1)}, f32[512,128]{0,1:T(8,128)}, u32[]{:S(2)}) copy-start(f32[512,128]{0,1:T(8,128)} %get-tuple-element.458) | copy-start | bytes 786436
  104.5 173.4 %copy-start.2 = (f32[512,128]{1,0:T(8,128)}, f32[512,128]{1,0:T(8,128)S(1)}, u32[]{:S(2)}) copy-start(f32[512,128]{1,0:T(8,128)S(1)} %copy.250.c_part) | copy-start | bytes 786436
  113.4 5.4 %copy-start.27 = (bf16[1024,64]{0,1:T(8,128)(2,1)}, bf16[1024,64]{0,1:T(8,128)(2,1)S(1)}, u32[]{:S(2)}) copy-start(bf16[1024,64]{0,1:T(8,128)(2,1)S(1)} %get-tuple-element.844) | copy-start | bytes 393220
  157.3 96.9 %all-reduce.8.cloned.1.call-start = ((), (), s32[]{:S(2)}) async-start(), calls=%async_computation.5 | async-start | bytes 4194304 | tf_op jit(solution)/shard_map/psum | solution.py:367
  202.2 3.5 copy-start.51
  202.2 163.9 %reduce-scatter.7.cloned.1.call-start = ((), (), s32[]{:S(2)}) async-start(), calls=%async_computation.8 | async-start | bytes 4718592
  259.6 4.4 copy-start.15
  267.1 10.7 %copy-start = (f32[512,384]{1,0:T(8,128)}, f32[512,384]{1,0:T(8,128)S(1)}, u32[]{:S(2)}) copy-start(f32[512,384]{1,0:T(8,128)S(1)} %copy.256.dgated) | copy-start | bytes 2359300
  277.7 3.8 copy-start.50
  277.8 134.5 %all-reduce.10.cloned.1.call-start = ((), (), s32[]{:S(2)}) async-start(), calls=%async_computation.6 | async-start | bytes 3145728 | tf_op jit(solution)/shard_map/psum | solution.py:510
  333.6 6.7 %copy-start.48 = (f32[32]{0:T(128)S(1)}, f32[32]{0:T(128)}, u32[]{:S(2)}) copy-start(f32[32]{0:T(128)} %copy-done.47) | copy-start | bytes 388
  369.5 127.2 %reduce-scatter.5.cloned.1.call-start = ((), (), s32[]{:S(2)}) async-start(), calls=%async_computation.7 | async-start | bytes 3538944 | tf_op jit(solution)/shard_map/reduce_scatter | solution.py:539
  369.8 45.5 %copy-start.14 = (bf16[1,512,1024]{2,1,0:T(8,128)(2,1)S(1)}, bf16[1,512,1024]{2,1,0:T(8,128)(2,1)}, u32[]{:S(2)}) copy-start(bf16[1,512,1024]{2,1,0:T(8,128)(2,1)} %param.24) | copy-start | bytes 3145732
  369.8 45.5 %copy-start.44 = (f32[512]{0:T(512)S(1)}, f32[512]{0:T(512)}, u32[]{:S(2)}) copy-start(f32[512]{0:T(512)} %copy-done.43) | copy-start | bytes 6148
  413.3 4.2 copy-start.49
  422.0 11.4 %copy-start.16 = (f32[512,1024]{1,0:T(8,128)S(1)}, f32[512,1024]{1,0:T(8,128)}, u32[]{:S(2)}) copy-start(f32[512,1024]{1,0:T(8,128)} %copy-done.15) | copy-start | bytes 6291460
  422.1 11.4 %copy-start.45 = (f32[512]{0:T(512)S(1)}, f32[512]{0:T(512)}, u32[]{:S(2)}) copy-start(f32[512]{0:T(512)} %get-tuple-element.488) | copy-start | bytes 6148
  496.6 4.5 copy-start.23
  (37 other events, 62.3 us)
Sparse Core Ops, SparseCore 0:
  15.4 62.8 all-gather.3
  81.0 73.2 all-gather.5
  157.4 34.2 all-reduce.5
  202.3 51.7 all-reduce.7
  277.9 88.1 reduce-scatter.6
  369.6 42.6 all-reduce.9
  422.2 74.4 reduce-scatter.4
